TPU v7x, 512 devices: a whole 4x4x16 slice. The times are simulated.
512 devices in a mesh: seq: 64 (over y, z_lo, core), chan: 8 (over x, z_hi).
Axes of the slice: x: 4, y: 4, z: 16 (z_hi: 2, z_lo: 8; z = z_hi * 8 + z_lo), core: 2. Of those that a mesh axis runs over, the one named last changes fastest.
Arguments:
- queries: bfloat16 [16384, 4096], P('seq', 'chan'), may hold values from -6 to 6
- key_proj: bfloat16 [16384, 4096], P('seq', 'chan'), may hold values from -6 to 6
- value_proj: bfloat16 [16384, 4096], P('seq', 'chan'), may hold values from -6 to 6
- decay_rate: float32 [4096, 16], P('chan'), may hold values from 1 to 546
- residues: float32 [4096, 16], P('chan'), may hold values from -1 to 1
- skip_gain: float32 [4096], P('chan'), may hold values from -1 to 1
- out_weight: bfloat16 [4096, 4096], P('chan'), may hold values from -0.125 to 0.125
Outputs:
- layer_out: bfloat16 [16384, 4096], P('seq', 'chan')
All inputs are finite; a program needn't handle non-finite values.
Results may differ from a plain program's by a relative error of at most 0.0049.
Values sent between devices are 32-bit elements; how exact they have to be, the bound alone decides.
No kernel may reach another device: no remote copies, remote signals or barrier semaphores. Data moves between devices by JAX's collectives and lax.ppermute only.
A program may use at most 128 MiB of HBM per device.

v0:
```python
import math

import jax
import jax.numpy as jnp
from jax import lax
from jax.sharding import PartitionSpec as P

HIGHEST_PREC = lax.Precision.HIGHEST


def phase_table(row_index, col_index, modulus):
    product = row_index[:, None] * col_index[None, :] % modulus
    angles = 2.0 * math.pi / modulus * product.astype(jnp.float32)
    return (jnp.cos(angles), jnp.sin(angles))


def build_filter(decay_rate, residues, positions, length):

    def add_mode(mode, totals):
        rate_col = lax.dynamic_slice_in_dim(decay_rate, mode, 1, 1)[:, 0]
        weight_col = lax.dynamic_slice_in_dim(residues, mode, 1, 1)[:, 0]
        coefficient = weight_col * jnp.sqrt(2.0 * rate_col / length)
        return totals + coefficient[None, :] * jnp.exp(
            -positions[:, None] * (rate_col[None, :] / length)
        )

    start = jnp.zeros((positions.shape[0], decay_rate.shape[0]), jnp.float32)
    return lax.fori_loop(0, decay_rate.shape[1], add_mode, start)


def per_device(queries, key_proj, value_proj, decay_rate, residues, skip_gain, out_weight):
    seq_size = lax.axis_size("seq")
    seq_index = lax.axis_index("seq")
    tok_rows, chans = queries.shape
    group_len = tok_rows // seq_size
    radix_len = 2 * seq_size
    length = tok_rows * seq_size
    total_len = 2 * length
    mixed_in = key_proj.astype(jnp.float32) * value_proj.astype(jnp.float32)
    cos_outer, sin_outer = phase_table(jnp.arange(radix_len), jnp.arange(seq_size), radix_len)
    spread_pos = seq_index * group_len + jnp.arange(group_len)
    twist_cos, twist_sin = phase_table(jnp.arange(radix_len), spread_pos, total_len)
    cos_inner, sin_inner = phase_table(jnp.arange(tok_rows), jnp.arange(tok_rows), tok_rows)
    own_low = 2 * seq_index + jnp.arange(2)
    positions = (seq_index * tok_rows + jnp.arange(tok_rows)).astype(jnp.float32)
    filter_time = build_filter(decay_rate, residues, positions, length)
    fields = jnp.stack([mixed_in, filter_time])
    shaped = fields.reshape(fields.shape[0], 1, tok_rows, chans)
    block_in = lax.all_to_all(shaped, "seq", split_axis=2, concat_axis=1, tiled=True)
    real_part = jnp.einsum("kn,fngc->fkgc", cos_outer, block_in, precision=HIGHEST_PREC)
    imag_part = -jnp.einsum("kn,fngc->fkgc", sin_outer, block_in, precision=HIGHEST_PREC)
    wave_cos = twist_cos[None, :, :, None]
    wave_sin = twist_sin[None, :, :, None]
    spread = jnp.stack(
        [real_part * wave_cos + imag_part * wave_sin, imag_part * wave_cos - real_part * wave_sin],
        axis=1,
    )
    block_in = lax.all_to_all(spread, "seq", split_axis=2, concat_axis=3, tiled=True)
    real_in = block_in[:, 0]
    imag_in = block_in[:, 1]
    real_part = jnp.einsum(
        "kn,fanc->fakc", cos_inner, real_in, precision=HIGHEST_PREC
    ) + jnp.einsum("kn,fanc->fakc", sin_inner, imag_in, precision=HIGHEST_PREC)
    imag_part = jnp.einsum(
        "kn,fanc->fakc", cos_inner, imag_in, precision=HIGHEST_PREC
    ) - jnp.einsum("kn,fanc->fakc", sin_inner, real_in, precision=HIGHEST_PREC)
    spectra = jnp.stack([real_part, imag_part], axis=1)
    input_spec = spectra[0]
    filter_spec = spectra[1]
    prod_real = input_spec[0] * filter_spec[0] - input_spec[1] * filter_spec[1]
    prod_imag = input_spec[0] * filter_spec[1] + input_spec[1] * filter_spec[0]
    back_real = jnp.einsum(
        "kn,akc->anc", cos_inner, prod_real, precision=HIGHEST_PREC
    ) - jnp.einsum("kn,akc->anc", sin_inner, prod_imag, precision=HIGHEST_PREC)
    back_imag = jnp.einsum(
        "kn,akc->anc", cos_inner, prod_imag, precision=HIGHEST_PREC
    ) + jnp.einsum("kn,akc->anc", sin_inner, prod_real, precision=HIGHEST_PREC)
    undo_cos, undo_sin = phase_table(own_low, jnp.arange(tok_rows), total_len)
    undo_cos = undo_cos[:, :, None]
    undo_sin = undo_sin[:, :, None]
    stacked = jnp.stack(
        [back_real * undo_cos - back_imag * undo_sin, back_real * undo_sin + back_imag * undo_cos]
    )
    block_in = lax.all_to_all(stacked, "seq", split_axis=2, concat_axis=1, tiled=True)
    summed = jnp.einsum("kn,kgc->ngc", cos_outer, block_in[0], precision=HIGHEST_PREC) - jnp.einsum(
        "kn,kgc->ngc", sin_outer, block_in[1], precision=HIGHEST_PREC
    )
    by_class = summed / total_len
    conv = lax.all_to_all(by_class, "seq", split_axis=0, concat_axis=1, tiled=True).reshape(
        tok_rows, chans
    )
    gated = (queries.astype(jnp.float32) * (conv + skip_gain[None, :] * mixed_in)).astype(
        jnp.bfloat16
    )
    partial_sums = jnp.dot(gated, out_weight, preferred_element_type=jnp.float32)
    return lax.psum_scatter(partial_sums, "chan", scatter_dimension=1, tiled=True).astype(
        jnp.bfloat16
    )


def solution(mesh):
    in_specs = (
        P("seq", "chan"),
        P("seq", "chan"),
        P("seq", "chan"),
        P("chan", None),
        P("chan", None),
        P("chan"),
        P("chan", None),
    )
    out_specs = P("seq", "chan")
    return jax.shard_map(
        per_device, mesh=mesh, in_specs=in_specs, out_specs=out_specs, check_vma=False
    )
```

profile of v0, /device:TPU:6, one launch (start us, length us, event | category | flops | bytes accessed | tf_op | source)
XLA Modules:
  0.0 714.3 jit_solution(17954688104597122338)
XLA Ops:
  6.5 16.2 %while.16 = (s32[]{:T(128)}, f32[256,512]{1,0:T(8,128)S(1)}, f32[512,16]{0,1:T(8,128)}, f32[512,16]{0,1:T(8,128)}, s32[]{:T(128)}, /*index=5*/s32[]{:T(128)}, s32[]{:T(128)}) while((s32[]{:T(128)}, f32[256,512]{1,0:T(8,128)S(1)}, f32[512,16]{0,1:T(8,128)}, f32[512,16]{0,1:T(8,128)}, s32[]{:T(128)}, /*index=5*/s32[]{:T(128)}, ...), condition=%wide.region_1.2_spmd.clone, body=%wide.region_0.1_spmd.clone.sunk | while | flops 526595 | bytes 1063007 | solution.py:28
  6.5 0.8 sqrt_multiply_fusion.2
  22.9 1.8 copy.22
  24.7 16.2 %all-to-all-start = ((f32[2,1,256,512]{3,0,1,2:T(2,128)}), f32[2,1,256,512]{3,0,1,2:T(2,128)S(1)}, u32[]{:S(2)}, u32[]{:S(2)}) async-start(f32[2,1,256,512]{3,0,1,2:T(2,128)} %copy.22), calls=%async_computation | async-start | bytes 2097152 | tf_op jit(solution)/shard_map/all_to_all | solution.py:49
  41.0 51.3 %all-to-all-done = f32[2,1,256,512]{3,0,1,2:T(2,128)S(1)} async-done(((f32[2,1,256,512]{3,0,1,2:T(2,128)}), f32[2,1,256,512]{3,0,1,2:T(2,128)S(1)}, u32[]{:S(2)}, u32[]{:S(2)}) %all-to-all-start) | async-done | bytes 1048608 | tf_op jit(solution)/shard_map/all_to_all | solution.py:49
  92.3 3.9 fusion.25
  96.1 3.9 fusion.11
  100.1 2.3 pad_maximum_fusion
  102.3 5.5 copy.25
  107.8 8.3 %all-to-all-start.1 = ((f32[2,2,128,4,512]{4,3,0,1,2:T(4,128)}), f32[2,2,128,4,512]{4,3,0,1,2:T(4,128)}, u32[]{:S(2)}, u32[]{:S(2)}) async-start(f32[2,2,128,4,512]{4,3,0,1,2:T(4,128)} %copy.25), calls=%async_computation.1 | async-start | bytes 8388608 | tf_op jit(solution)/shard_map/all_to_all | solution.py:58
  116.8 181.6 %all-to-all-done.1 = f32[2,2,128,4,512]{4,3,0,1,2:T(4,128)} async-done(((f32[2,2,128,4,512]{4,3,0,1,2:T(4,128)}), f32[2,2,128,4,512]{4,3,0,1,2:T(4,128)}, u32[]{:S(2)}, u32[]{:S(2)}) %all-to-all-start.1) | async-done | bytes 4194336 | tf_op jit(solution)/shard_map/all_to_all | solution.py:58
  298.4 5.4 copy.27
  303.9 3.4 fusion.131
  307.3 2.8 copy.41
  310.0 4.1 fusion.4
  314.2 4.1 fusion.2
  318.2 2.9 copy.40
  321.2 4.7 add_bitcast_fusion
  325.9 2.9 subtract_bitcast_fusion
  329.1 2.0 fusion.19
  331.1 2.0 fusion.23
  333.1 2.2 convolution_add_fusion
  335.3 2.1 subtract_bitcast_fusion.1
  337.5 2.4 copy.30
  339.9 106.5 %all_to_all.54 = f32[2,2,256,512]{3,1,0,2:T(2,128)S(1)} all-to-all(f32[2,2,256,512]{3,1,0,2:T(2,128)} %copy.30), channel_id=1, replica_groups=mesh['seq'=64,'chan'=8] {'seq'}, dimensions={2} | all-to-all | bytes 4194304 | tf_op jit(solution)/shard_map/all_to_all | solution.py:84
  447.2 0.8 fusion.132
  449.1 1.6 fusion.62
  452.1 0.8 fusion.18
  453.3 40.1 %all_to_all.55 = f32[64,4,512]{2,1,0:T(4,128)S(1)} all-to-all(f32[64,4,512]{2,1,0:T(4,128)S(1)} %copy.34), channel_id=1, replica_groups=mesh['seq'=64,'chan'=8] {'seq'}, dimensions={0} | all-to-all | bytes 1048576 | tf_op jit(solution)/shard_map/all_to_all | solution.py:89
  493.6 5.4 fusion.33
  499.0 206.4 %reduce-scatter.2.cloned.1.call-done = f32[256,512]{1,0:T(8,128)} async-done(((f32[256,4096]{1,0:T(8,128)}), f32[256,512]{1,0:T(8,128)}) %reduce-scatter.2.cloned.1.call-update) | async-done | bytes 524304 | tf_op jit(solution)/shard_map/reduce_scatter | solution.py:96
  705.4 1.8 convert_element_type.78
  (79 shorter events, 19.9 us)
Async XLA Ops:
  6.5 16.2 %copy-start.2 = (bf16[256,512]{1,0:T(8,128)(2,1)S(1)}, bf16[256,512]{1,0:T(8,128)(2,1)}, u32[]{:S(2)}) copy-start(bf16[256,512]{1,0:T(8,128)(2,1)} %param.11) | copy-start | bytes 786436
  6.5 16.2 %copy-start.3 = (bf16[256,512]{1,0:T(8,128)(2,1)S(1)}, bf16[256,512]{1,0:T(8,128)(2,1)}, u32[]{:S(2)}) copy-start(bf16[256,512]{1,0:T(8,128)(2,1)} %param.10) | copy-start | bytes 786436
  24.7 67.6 %all-to-all-start = ((f32[2,1,256,512]{3,0,1,2:T(2,128)}), f32[2,1,256,512]{3,0,1,2:T(2,128)S(1)}, u32[]{:S(2)}, u32[]{:S(2)}) async-start(f32[2,1,256,512]{3,0,1,2:T(2,128)} %copy.22), calls=%async_computation | async-start | bytes 2097152 | tf_op jit(solution)/shard_map/all_to_all | solution.py:49
  107.8 190.6 %all-to-all-start.1 = ((f32[2,2,128,4,512]{4,3,0,1,2:T(4,128)}), f32[2,2,128,4,512]{4,3,0,1,2:T(4,128)}, u32[]{:S(2)}, u32[]{:S(2)}) async-start(f32[2,2,128,4,512]{4,3,0,1,2:T(4,128)} %copy.25), calls=%async_computation.1 | async-start | bytes 8388608 | tf_op jit(solution)/shard_map/all_to_all | solution.py:58
  116.2 589.3 %reduce-scatter.2.cloned.1.call-start = ((), (), s32[]{:S(2)}) async-start(), calls=%async_computation.5 | async-start | bytes 4718592 | tf_op jit(solution)/shard_map/reduce_scatter | solution.py:96
  321.2 4.7 copy-start
  451.0 1.0 copy-start.1
  452.9 40.7 %copy-start.4 = (bf16[256,512]{1,0:T(8,128)(2,1)S(1)}, bf16[256,512]{1,0:T(8,128)(2,1)}, u32[]{:S(2)}) copy-start(bf16[256,512]{1,0:T(8,128)(2,1)} %param.10) | copy-start | bytes 786436
  452.9 40.7 %copy-start.5 = (bf16[256,512]{1,0:T(8,128)(2,1)S(1)}, bf16[256,512]{1,0:T(8,128)(2,1)}, u32[]{:S(2)}) copy-start(bf16[256,512]{1,0:T(8,128)(2,1)} %param.9) | copy-start | bytes 786436
  452.9 40.7 %copy-start.6 = (f32[512]{0:T(512)S(1)}, f32[512]{0:T(512)}, u32[]{:S(2)}) copy-start(f32[512]{0:T(512)} %param.14) | copy-start | bytes 6148
Sparse Core Ops, SparseCore 0:
  499.2 206.2 reduce-scatter.1
where the time goes:
time: 726 us; the launch traced here: 714 us
  waiting for transfers between devices  439 us (60%)
  blocking collectives  147 us (20%)
  matrix products  39.7 us (5%)
  local copies, waits for them, and re-layouts  28.7 us (4%)
  starting transfers between devices  25 us (3%)
  other arithmetic  20.5 us (3%)
  between operations  13.9 us (2%)
    reduce_scatter x1, waiting for transfers between devices, per_device(): lax.psum_scatter(partial_sums, 'chan', scatter_dimension=1, tiled=True)  206 us
    all_to_all x1, waiting for transfers between devices, per_device(): lax.all_to_all(spread, 'seq', split_axis=2, concat_axis=3, tiled=True)  182 us
    all_to_all x1, blocking collectives, per_device(): lax.all_to_all(stacked, 'seq', split_axis=2, concat_axis=1, tiled=True)  107 us
    all_to_all x1, waiting for transfers between devices, per_device(): lax.all_to_all(shaped, 'seq', split_axis=2, concat_axis=1, tiled=True)  51.3 us
    all_to_all x1, blocking collectives, per_device(): lax.all_to_all(by_class, 'seq', split_axis=0, concat_axis=1, tiled=True)  40.1 us
    all_to_all x1, starting transfers between devices, per_device(): lax.all_to_all(shaped, 'seq', split_axis=2, concat_axis=1, tiled=True)  16.2 us
  transfers between devices with their start and end apart: 3, of which 3 were waited for; matrix products, arithmetic and copies ran while one was open for 0% of the time, Pallas kernels for 0%

commit v1 on v0

v1 whole, which is shorter than its diff:
```python
import functools

import jax
import jax.numpy as jnp
from jax import lax
from jax.experimental import pallas as pl
from jax.experimental.pallas import tpu as pltpu
from jax.sharding import Mesh
from jax.sharding import PartitionSpec as P

F32 = jnp.float32
LANES = 128
SUBS = 8
ALL_VMEM = 56 * 1024 * 1024
MOST_VMEM = 52 * 1024 * 1024
CHUNKS = 2
SEQ_PARTS = (("y", 4), ("zl", 8), ("core", 2))
CHAN_PARTS = (("x", 4), ("zh", 2))
SEQ = tuple(name for name, _ in SEQ_PARTS)
CHAN = tuple(name for name, _ in CHAN_PARTS)


def tree_sum(terms):
    while len(terms) > 1:
        terms = [a + b for a, b in zip(terms[::2], terms[1::2])]
    return terms[0]


def whole_call(kernel, out_shape, scratch_shapes, vmem, args, in_specs=None):
    return pl.pallas_call(
        kernel,
        in_specs=in_specs or [pl.BlockSpec(memory_space=pltpu.VMEM)] * len(args),
        out_specs=jax.tree.map(lambda _: pl.BlockSpec(memory_space=pltpu.VMEM), out_shape),
        out_shape=out_shape,
        scratch_shapes=scratch_shapes,
        compiler_params=pltpu.CompilerParams(vmem_limit_bytes=vmem),
        cost_estimate=pl.CostEstimate(flops=1 << 24, bytes_accessed=1 << 21, transcendentals=0),
    )(*args)


def mix_into(x_ref, k_ref, v_ref):
    tokens, chans = k_ref.shape
    for tile in range(chans // LANES):
        lanes = pl.ds(tile * LANES, LANES)
        x_ref[pl.ds(tile * tokens, tokens), :] = k_ref[:, lanes].astype(F32) * v_ref[:, lanes].astype(F32)


def spread_row(ref, row, lanes):
    return jnp.broadcast_to(ref[row : row + 1, lanes], (SUBS, LANES))


def state_kernel(length, *refs):
    hbm, refs = refs[:4], refs[4:]
    rate_ref, coef_ref, ends_ref, state_ref, fade_ref, x_ref, *arrived, sems = refs
    copies = [pltpu.make_async_copy(src, dst, sems.at[i]) for i, (src, dst) in enumerate(zip(hbm, arrived))]
    for copy in copies:
        copy.start()
    for copy in copies:
        copy.wait()
    k_ref, v_ref, decay_ref, res_ref = arrived
    tokens, chans = k_ref.shape
    modes = rate_ref.shape[0]
    run = tokens // SUBS
    mix_into(x_ref, k_ref, v_ref)
    rate = decay_ref[...] / length
    rate_ref[...] = rate
    coef_ref[...] = res_ref[...] * jnp.sqrt(2.0 * rate)
    later = (SUBS - 1 - lax.broadcasted_iota(jnp.int32, (SUBS, LANES), 0)).astype(F32) * run
    for tile in range(chans // LANES):
        lanes = pl.ds(tile * LANES, LANES)
        rates = [spread_row(rate_ref, m, lanes) for m in range(modes)]
        steps = [jnp.exp(-r) for r in rates]

        def body(j, held, base=tile * tokens):
            x = x_ref[pl.ds(base + j, SUBS, stride=run), :]
            return tuple(a * h + x for a, h in zip(steps, held))

        held = tuple(jnp.zeros((SUBS, LANES), F32) for _ in range(modes))
        held = lax.fori_loop(0, run, body, held, unroll=8)
        for m in range(modes):
            ends_ref[m, :, lanes] = held[m]
            row = m * (chans // LANES) + tile
            state_ref[row : row + 1, :] = jnp.sum(held[m] * jnp.exp(-rates[m] * later), axis=0, keepdims=True)
            fade_ref[row : row + 1, :] = jnp.exp(-rates[m][:1] * tokens)


def local_kernel(x_ref, rate_ref, coef_ref, ends_ref, skip_ref, out_ref, y_ref):
    chans = rate_ref.shape[1]
    tokens = x_ref.shape[0] * LANES // chans
    modes = rate_ref.shape[0]
    run = tokens // SUBS
    place = lax.broadcasted_iota(jnp.int32, (SUBS, LANES), 0)

    def down(value, by):
        return jnp.where(place >= by, pltpu.roll(value, by, 0), 0.0)

    for tile in range(chans // LANES):
        lanes = pl.ds(tile * LANES, LANES)
        steps, held = [], []
        for m in range(modes):
            rate = spread_row(rate_ref, m, lanes)
            steps.append(jnp.exp(-rate))
            total = ends_ref[m, :, lanes]
            for by in (1, 2, 4):
                total = total + jnp.exp(-rate * (by * run)) * down(total, by)
            held.append(down(total, 1))
        coefs = [spread_row(coef_ref, m, lanes) for m in range(modes)]

        def body(j, held, base=tile * tokens):
            x = x_ref[pl.ds(base + j, SUBS, stride=run), :]
            held = tuple(a * h + x for a, h in zip(steps, held))
            y_ref[pl.ds(base + j, SUBS, stride=run), :] = tree_sum([c * h for c, h in zip(coefs, held)])
            return held

        lax.fori_loop(0, run, body, tuple(held), unroll=4)
        rows = pl.ds(tile * tokens, tokens)
        out_ref[rows, :] = y_ref[rows, :] + skip_ref[:, lanes] * x_ref[rows, :]


def gate_kernel(q_ref, local_ref, rate_ref, coef_ref, enter_ref, out_ref, y_ref):
    tokens, chans = q_ref.shape
    modes = rate_ref.shape[0]
    run = tokens // SUBS
    place = (lax.broadcasted_iota(jnp.int32, (SUBS, LANES), 0) * run + 1).astype(F32)
    for tile in range(chans // LANES):
        lanes = pl.ds(tile * LANES, LANES)
        steps, held = [], []
        for m in range(modes):
            rate = spread_row(rate_ref, m, lanes)
            steps.append(jnp.exp(-rate))
            weight = spread_row(coef_ref, m, lanes) * spread_row(enter_ref, m * (chans // LANES) + tile, slice(None))
            held.append(weight * jnp.exp(-rate * place))

        def body(j, held, base=tile * tokens):
            y_ref[pl.ds(base + j, SUBS, stride=run), :] = tree_sum(list(held))
            return tuple(a * h for a, h in zip(steps, held))

        lax.fori_loop(0, run, body, tuple(held), unroll=4)
        rows = pl.ds(tile * tokens, tokens)
        value = q_ref[:, lanes].astype(F32) * (local_ref[rows, :] + y_ref[rows, :])
        out_ref[:, lanes] = value.astype(out_ref.dtype)


def project_kernel(adds, joined, width, cols_ref, gated_ref, weight_ref, *refs):
    terms, outs, (block_ref, sems) = refs[: len(adds)], refs[len(adds) : -2], refs[-2:]
    fetches = start_fetches(cols_ref, width, weight_ref, block_ref, sems)
    for half in range(2):
        fetches[half].wait()
        block = jnp.dot(gated_ref[...], block_ref[half], preferred_element_type=F32)
        for which, term in zip(adds, terms):
            if which == half:
                block = block + term[...]
        if joined:
            outs[0][half] = block
        else:
            outs[half][...] = block


def own_kernel(width, cols_ref, gated_ref, weight_ref, left_ref, right_ref, keep_ref, send_ref, block_ref, sems):
    fetches = start_fetches(cols_ref, width, weight_ref, block_ref, sems)
    mine = cols_ref[2]
    for half, at, out in ((1, 1 - mine, send_ref), (0, mine, keep_ref)):
        fetches[half].wait()
        block = jnp.dot(gated_ref[...], block_ref[half], preferred_element_type=F32)
        out[...] = block + left_ref[at] + right_ref[at]


def start_fetches(cols_ref, width, weight_ref, block_ref, sems):
    fetches = []
    for half in range(2):
        lanes = pl.ds(pl.multiple_of(cols_ref[half] * width, LANES), width)
        fetches.append(pltpu.make_async_copy(weight_ref.at[:, lanes], block_ref.at[half], sems.at[half]))
        fetches[-1].start()
    return fetches


def project_call(kernel, shapes, width, cols, gated, weight, terms):
    vmem = pl.BlockSpec(memory_space=pltpu.VMEM)
    return pl.pallas_call(
        kernel,
        in_specs=[pl.BlockSpec(memory_space=pltpu.SMEM), vmem, pl.BlockSpec(memory_space=pl.ANY)] + [vmem] * len(terms),
        out_specs=[vmem] * len(shapes),
        out_shape=shapes,
        scratch_shapes=[pltpu.VMEM((2, weight.shape[0], width), weight.dtype), pltpu.SemaphoreType.DMA((2,))],
        compiler_params=pltpu.CompilerParams(vmem_limit_bytes=MOST_VMEM),
        cost_estimate=pl.CostEstimate(flops=1 << 27, bytes_accessed=1 << 20, transcendentals=0),
    )(cols, gated, weight, *terms)


def project(gated, weight, cols, width, adds=(), terms=(), joined=False):
    tokens = gated.shape[0]
    if joined:
        shapes = (jax.ShapeDtypeStruct((2, tokens, width), F32),)
    else:
        shapes = (jax.ShapeDtypeStruct((tokens, width), F32),) * 2
    outs = project_call(functools.partial(project_kernel, adds, joined, width), shapes, width, cols, gated, weight, terms)
    return outs[0] if joined else outs


def project_own(gated, weight, cols, width, z_index, terms):
    cols = jnp.concatenate([cols, z_index.astype(jnp.int32)[None]])
    shapes = (jax.ShapeDtypeStruct((gated.shape[0], width), F32),) * 2
    return project_call(functools.partial(own_kernel, width), shapes, width, cols, gated, weight, terms)


def shift(value, axis, by):
    size = lax.axis_size(axis)
    return lax.ppermute(value, axis, [(i, (i + by) % size) for i in range(size)])


def scan_kernel(state_ref, fade_ref, enter_ref):
    count, total = fade_ref.shape[0], jnp.zeros(fade_ref.shape, F32)
    for first in range(0, state_ref.shape[0], count):
        enter_ref[first : first + count, :] = total
        total = total * fade_ref[...] + state_ref[first : first + count, :]


def entering_states(state, fade):
    count, index = state.shape[0], jnp.int32(0)
    for axis in SEQ:
        count = count // lax.axis_size(axis)
        index = index * lax.axis_size(axis) + lax.axis_index(axis)
    fade = lax.dynamic_slice_in_dim(fade, index * count, count, 0)
    state = lax.all_to_all(state, SEQ, 0, 0, tiled=True)
    enter = whole_call(scan_kernel, jax.ShapeDtypeStruct(state.shape, F32), [], MOST_VMEM, (state, fade))
    return lax.all_to_all(enter, SEQ, 0, 0, tiled=True)


def per_device(queries, key_proj, value_proj, decay_rate, residues, skip_gain, out_weight):
    tokens, chans = queries.shape
    modes = decay_rate.shape[1]
    seq_size = 1
    for axis in SEQ:
        seq_size *= lax.axis_size(axis)
    small = jax.ShapeDtypeStruct((modes, chans), F32)
    stacked = jax.ShapeDtypeStruct((tokens * chans // LANES, LANES), F32)
    args = (key_proj, value_proj, decay_rate.T, residues.T)
    ends = jax.ShapeDtypeStruct((modes, SUBS, chans), F32)
    rows = jax.ShapeDtypeStruct((modes * chans // LANES, LANES), F32)
    rate, coef, ends, state, fade, mixed = whole_call(
        functools.partial(state_kernel, float(tokens * seq_size)),
        (small, small, ends, rows, rows, stacked),
        [pltpu.VMEM(a.shape, a.dtype) for a in args] + [pltpu.SemaphoreType.DMA((len(args),))],
        ALL_VMEM,
        args,
        [pl.BlockSpec(memory_space=pl.ANY)] * len(args),
    )
    scratch = [pltpu.VMEM(stacked.shape, F32)]
    local = whole_call(local_kernel, stacked, scratch, ALL_VMEM, (mixed, rate, coef, ends, skip_gain[None, :]))
    enter = entering_states(state, fade)
    gated = jax.ShapeDtypeStruct((tokens, chans), queries.dtype)
    gated = whole_call(gate_kernel, gated, scratch, ALL_VMEM, (queries, local, rate, coef, enter))

    x_size, x_index = lax.axis_size("x"), lax.axis_index("x")
    z_size, z_index = lax.axis_size("zh"), lax.axis_index("zh")
    features = out_weight.shape[1] // (x_size * z_size)
    width = features // CHUNKS

    def cols(x_by, first, chunk):
        start = ((x_index + x_by) % x_size) * z_size
        return ((start + jnp.stack([first, 1 - first])) * CHUNKS + chunk).astype(jnp.int32)

    zero = jnp.int32(0)
    outs, summed, kept, swapped = [], [], [], []
    for chunk in range(CHUNKS + 2):
        if chunk < CHUNKS:
            behind = summed[chunk - 2 :] + kept[chunk - 3 :] if chunk >= 2 else []
            source, *_ = lax.optimization_barrier((gated, *behind))
            far = project(source, out_weight, cols(2, zero, chunk), width)
            summed.append((shift(far[0], "x", 1), shift(far[1], "x", -1)))
        if 1 <= chunk <= CHUNKS:
            at = chunk - 1
            from_left, from_right = summed[at]
            source, *_ = lax.optimization_barrier((gated, *swapped[at - 3 :])) if at >= 3 else (gated,)
            right = project(source, out_weight, cols(1, zero, at), width, (0,), (from_left,), True)
            left = project(source, out_weight, cols(-1, zero, at), width, (1,), (from_right,), True)
            summed[at] = (right, left)
        if chunk >= 2:
            at = chunk - 2
            right, left = summed[at]
            terms = (shift(right, "x", 1), shift(left, "x", -1))
            keep, send = project_own(gated, out_weight, cols(0, z_index, at), width, z_index, terms)
            kept.append(send)
            swapped.append(shift(send, "zh", 1))
            outs.append(keep + swapped[at])
    return jnp.concatenate(outs, axis=1).astype(jnp.bfloat16)


def solution(mesh):
    sizes = [size for _, size in SEQ_PARTS + CHAN_PARTS]
    parts = Mesh(mesh.devices.reshape(sizes), SEQ + CHAN)
    in_specs = (
        P(SEQ, CHAN),
        P(SEQ, CHAN),
        P(SEQ, CHAN),
        P(CHAN, None),
        P(CHAN, None),
        P(CHAN),
        P(CHAN, None),
    )
    return jax.shard_map(
        per_device, mesh=parts, in_specs=in_specs, out_specs=P(SEQ, CHAN), check_vma=False
    )
```

time: 726 us -> 154 us (0.21)
  the two profiles are of different devices: /device:TPU:6 before, /device:TPU:33 now
where the time goes in v1:
time: 154 us; the launch traced here: 153 us
  starting transfers between devices  62.5 us (41%)
  waiting for transfers between devices  58.2 us (38%)
  Pallas kernels  28.5 us (19%)
  local copies, waits for them, and re-layouts  2.24 us (1%)
    ppermute x10, waiting for transfers between devices, shift(): lax.ppermute(value, axis, [(i, (i + by) % size) for i in range(size)])  41 us
    ppermute x10, starting transfers between devices, shift(): lax.ppermute(value, axis, [(i, (i + by) % size) for i in range(size)])  40.4 us
    pallas_call x8, Pallas kernels, project_call(): pl.pallas_call(kernel, in_specs=[pl.BlockSpec(memory_space=pltpu.SMEM), v...  18.1 us
    all_to_all x1, starting transfers between devices, entering_states(): state = lax.all_to_all(state, SEQ, 0, 0, tiled=True)  16.1 us
    pallas_call x4, Pallas kernels, whole_call(): pl.pallas_call(kernel, in_specs=in_specs or [pl.BlockSpec(memory_space=pl...  10.4 us
    all_to_all x1, waiting for transfers between devices, entering_states(): state = lax.all_to_all(state, SEQ, 0, 0, tiled=True)  10.2 us
    all_to_all x1, waiting for transfers between devices, entering_states(): return lax.all_to_all(enter, SEQ, 0, 0, tiled=True)  7 us
    all_to_all x1, starting transfers between devices, entering_states(): return lax.all_to_all(enter, SEQ, 0, 0, tiled=True)  6.03 us
  transfers between devices with their start and end apart: 12, of which 4 were waited for; matrix products, arithmetic and copies ran while one was open for 1% of the time, Pallas kernels for 13%

profile of v1, /device:TPU:33, one launch (start us, length us, event | category | flops | bytes accessed | tf_op | source)
XLA Modules:
  0.0 152.9 jit_solution(14228822744143565106)
XLA Ops:
  0.0 3.0 %shard_map.73 = (f32[16,512]{1,0:T(8,128)}, f32[16,512]{1,0:T(8,128)}, f32[16,8,512]{2,1,0:T(8,128)}, f32[64,128]{1,0:T(8,128)}, f32[64,128]{1,0:T(8,128)}, /*index=5*/f32[1024,128]{1,0:T(8,128)}) custom-call(bf16[256,512]{1,0:T(8,128)(2,1)} %refs_0_.1, bf16[256,512]{1,0:T(8,128)(2,1)} %refs_1_.1, f32[16,512]{1,0:T(8,128)} %bitcast.15, f32[16,512]{1,0:T(8,128)} %bitcast.16), custom_call_target="tpu_custom_call" | custom-call | flops 16777216 | bytes 2097152 | tf_op jit(solution)/shard_map/pallas_call | solution.py:30
  3.0 16.1 %all-to-all-start = ((f32[64,1,128]{2,1,0:T(1,128)}), f32[64,1,128]{2,1,0:T(1,128)S(1)}, u32[]{:S(2)}, u32[]{:S(2)}) async-start(f32[64,1,128]{2,1,0:T(1,128)} %bitcast.17), calls=%async_computation | async-start | bytes 65536 | tf_op jit(solution)/shard_map/all_to_all | solution.py:224
  19.2 0.7 constant_dynamic-slice_fusion.fade_ref
  19.8 10.2 %all-to-all-done = f32[64,1,128]{2,1,0:T(1,128)S(1)} async-done(((f32[64,1,128]{2,1,0:T(1,128)}), f32[64,1,128]{2,1,0:T(1,128)S(1)}, u32[]{:S(2)}, u32[]{:S(2)}) %all-to-all-start) | async-done | bytes 32800 | tf_op jit(solution)/shard_map/all_to_all | solution.py:224
  30.0 0.8 shard_map.75
  30.8 6.0 %all-to-all-start.1 = ((f32[64,1,128]{2,1,0:T(1,128)}), f32[64,1,128]{2,1,0:T(1,128)S(1)}, u32[]{:S(2)}, u32[]{:S(2)}) async-start(f32[64,1,128]{2,1,0:T(1,128)} %bitcast.9), calls=%async_computation.1 | async-start | bytes 65536 | tf_op jit(solution)/shard_map/all_to_all | solution.py:226
  36.8 4.0 %shard_map.74.local_ref = f32[1024,128]{1,0:T(8,128)} custom-call(f32[1024,128]{1,0:T(8,128)} %get-tuple-element.19.x_ref, f32[16,512]{1,0:T(8,128)} %get-tuple-element.20.rate_ref, f32[16,512]{1,0:T(8,128)} %get-tuple-element.21.coef_ref, f32[16,8,512]{2,1,0:T(8,128)} %get-tuple-element.22.ends_ref, f32[1,512]{1,0:T(1,128)} %bitcast.18), custom_call_target="tpu_custom_call" | custom-call | flops 16777216 | bytes 2097152 | tf_op jit(solution)/shard_map/pallas_call | solution.py:30
  40.8 7.0 %all-to-all-done.1 = f32[64,1,128]{2,1,0:T(1,128)S(1)} async-done(((f32[64,1,128]{2,1,0:T(1,128)}), f32[64,1,128]{2,1,0:T(1,128)S(1)}, u32[]{:S(2)}, u32[]{:S(2)}) %all-to-all-start.1) | async-done | bytes 32800 | tf_op jit(solution)/shard_map/all_to_all | solution.py:226
  47.8 0.6 copy-done.2
  48.4 2.7 %shard_map.76.gated_ref = bf16[256,512]{1,0:T(8,128)(2,1)} custom-call(bf16[256,512]{1,0:T(8,128)(2,1)} %q_ref.1, f32[1024,128]{1,0:T(8,128)} %shard_map.74.local_ref, f32[16,512]{1,0:T(8,128)} %get-tuple-element.20.rate_ref, f32[16,512]{1,0:T(8,128)} %get-tuple-element.21.coef_ref, f32[64,128]{1,0:T(8,128)} %bitcast.14), custom_call_target="tpu_custom_call" | custom-call | flops 16777216 | bytes 2097152 | tf_op jit(solution)/shard_map/pallas_call | solution.py:30
  51.1 0.9 copy-done
  52.1 2.1 %shard_map.81 = (f32[256,256]{1,0:T(8,128)S(1)}, f32[256,256]{1,0:T(8,128)S(1)}) custom-call(s32[2]{0:T(128)S(1)} %broadcast_add_fusion.1.cols_ref, bf16[256,512]{1,0:T(8,128)(2,1)S(1)} %copy-done, bf16[512,4096]{1,0:T(8,128)(2,1)} %weight_ref.15), custom_call_target="tpu_custom_call" | custom-call | flops 134217728 | bytes 1048576 | tf_op jit(solution)/shard_map/pallas_call | solution.py:179
  54.2 3.1 %collective-permute-start.5 = (f32[256,256]{1,0:T(8,128)S(1)}, f32[256,256]{1,0:T(8,128)S(1)}, u32[]{:S(2)}, u32[]{:S(2)}) collective-permute-start(f32[256,256]{1,0:T(8,128)S(1)} %get-tuple-element.29), channel_id=1, source_target_pairs={{0,2},{2,4},{4,6},{6,0},{1,3},{3,5},{5,7},{7,1},{8,10},{10,12},{12... | collective-permute-start | bytes 786440 | tf_op jit(solution)/shard_map/ppermute | solution.py:208
  57.3 3.4 %collective-permute-start.7 = (f32[256,256]{1,0:T(8,128)S(1)}, f32[256,256]{1,0:T(8,128)S(1)}, u32[]{:S(2)}, u32[]{:S(2)}) collective-permute-start(f32[256,256]{1,0:T(8,128)S(1)} %get-tuple-element.30), channel_id=1, source_target_pairs={{0,6},{2,0},{4,2},{6,4},{1,7},{3,1},{5,3},{7,5},{8,14},{10,8},{12,... | collective-permute-start | bytes 786440 | tf_op jit(solution)/shard_map/ppermute | solution.py:208
  60.7 2.1 %shard_map.77 = (f32[256,256]{1,0:T(8,128)S(1)}, f32[256,256]{1,0:T(8,128)S(1)}) custom-call(s32[2]{0:T(128)S(1)} %add_multiply_fusion.1.cols_ref, bf16[256,512]{1,0:T(8,128)(2,1)S(1)} %copy-done.1, bf16[512,4096]{1,0:T(8,128)(2,1)} %weight_ref.15), custom_call_target="tpu_custom_call" | custom-call | flops 134217728 | bytes 1048576 | tf_op jit(solution)/shard_map/pallas_call | solution.py:179
  62.8 1.9 %collective-permute-start = (f32[256,256]{1,0:T(8,128)S(1)}, f32[256,256]{1,0:T(8,128)S(1)}, u32[]{:S(2)}, u32[]{:S(2)}) collective-permute-start(f32[256,256]{1,0:T(8,128)S(1)} %get-tuple-element.25), channel_id=1, source_target_pairs={{0,2},{2,4},{4,6},{6,0},{1,3},{3,5},{5,7},{7,1},{8,10},{10,12},{12... | collective-permute-start | bytes 786440 | tf_op jit(solution)/shard_map/ppermute | solution.py:208
  64.8 4.6 %collective-permute-start.2 = (f32[256,256]{1,0:T(8,128)S(1)}, f32[256,256]{1,0:T(8,128)S(1)}, u32[]{:S(2)}, u32[]{:S(2)}) collective-permute-start(f32[256,256]{1,0:T(8,128)S(1)} %get-tuple-element.26), channel_id=1, source_target_pairs={{0,6},{2,0},{4,2},{6,4},{1,7},{3,1},{5,3},{7,5},{8,14},{10,8},{12,... | collective-permute-start | bytes 786440 | tf_op jit(solution)/shard_map/ppermute | solution.py:208
  69.4 2.1 %shard_map.82 = f32[2,256,256]{2,1,0:T(8,128)S(1)} custom-call(s32[2]{0:T(128)S(1)} %broadcast_add_fusion.2.cols_ref, bf16[256,512]{1,0:T(8,128)(2,1)S(1)} %copy-done.1, bf16[512,4096]{1,0:T(8,128)(2,1)} %weight_ref.15, f32[256,256]{1,0:T(8,128)S(1)} %collective-permute-done.5.refs_0_), custom_call_target="tpu_custom_call" | custom-call | flops 134217728 | bytes 1048576 | tf_op jit(solution)/shard_map/pallas_call | solution.py:179
  71.5 1.9 %collective-permute-start.6 = (f32[2,256,256]{2,1,0:T(8,128)S(1)}, f32[2,256,256]{2,1,0:T(8,128)S(1)}, u32[]{:S(2)}, u32[]{:S(2)}) collective-permute-start(f32[2,256,256]{2,1,0:T(8,128)S(1)} %shard_map.82), channel_id=1, source_target_pairs={{0,2},{2,4},{4,6},{6,0},{1,3},{3,5},{5,7},{7,1},{8,10},{10,12},{12... | collective-permute-start | bytes 1572872 | tf_op jit(solution)/shard_map/ppermute | solution.py:208
  73.4 2.1 %shard_map.83 = f32[2,256,256]{2,1,0:T(8,128)S(1)} custom-call(s32[2]{0:T(128)S(1)} %broadcast_add_fusion.cols_ref, bf16[256,512]{1,0:T(8,128)(2,1)S(1)} %copy-done.1, bf16[512,4096]{1,0:T(8,128)(2,1)} %weight_ref.15, f32[256,256]{1,0:T(8,128)S(1)} %collective-permute-done.7.refs_0_), custom_call_target="tpu_custom_call" | custom-call | flops 134217728 | bytes 1048576 | tf_op jit(solution)/shard_map/pallas_call | solution.py:179
  75.5 4.6 %collective-permute-start.8 = (f32[2,256,256]{2,1,0:T(8,128)S(1)}, f32[2,256,256]{2,1,0:T(8,128)S(1)}, u32[]{:S(2)}, u32[]{:S(2)}) collective-permute-start(f32[2,256,256]{2,1,0:T(8,128)S(1)} %shard_map.83), channel_id=1, source_target_pairs={{0,6},{2,0},{4,2},{6,4},{1,7},{3,1},{5,3},{7,5},{8,14},{10,8},{12,... | collective-permute-start | bytes 1572872 | tf_op jit(solution)/shard_map/ppermute | solution.py:208
  80.1 2.1 %shard_map.78 = f32[2,256,256]{2,1,0:T(8,128)S(1)} custom-call(s32[2]{0:T(128)S(1)} %add_multiply_fusion.2.cols_ref, bf16[256,512]{1,0:T(8,128)(2,1)S(1)} %copy-done.1, bf16[512,4096]{1,0:T(8,128)(2,1)} %weight_ref.15, f32[256,256]{1,0:T(8,128)S(1)} %collective-permute-done.refs_0_), custom_call_target="tpu_custom_call" | custom-call | flops 134217728 | bytes 1048576 | tf_op jit(solution)/shard_map/pallas_call | solution.py:179
  82.2 1.9 %collective-permute-start.1 = (f32[2,256,256]{2,1,0:T(8,128)S(1)}, f32[2,256,256]{2,1,0:T(8,128)S(1)}, u32[]{:S(2)}, u32[]{:S(2)}) collective-permute-start(f32[2,256,256]{2,1,0:T(8,128)S(1)} %shard_map.78), channel_id=1, source_target_pairs={{0,2},{2,4},{4,6},{6,0},{1,3},{3,5},{5,7},{7,1},{8,10},{10,12},{12... | collective-permute-start | bytes 1572872 | tf_op jit(solution)/shard_map/ppermute | solution.py:208
  84.1 2.9 %shard_map.79 = f32[2,256,256]{2,1,0:T(8,128)} custom-call(s32[2]{0:T(128)S(1)} %add_multiply_fusion.cols_ref, bf16[256,512]{1,0:T(8,128)(2,1)S(1)} %copy-done.1, bf16[512,4096]{1,0:T(8,128)(2,1)} %weight_ref.15, f32[256,256]{1,0:T(8,128)S(1)} %collective-permute-done.2.refs_0_), custom_call_target="tpu_custom_call" | custom-call | flops 134217728 | bytes 1048576 | tf_op jit(solution)/shard_map/pallas_call | solution.py:179
  87.0 4.6 %collective-permute-start.3 = (f32[2,256,256]{2,1,0:T(8,128)}, f32[2,256,256]{2,1,0:T(8,128)}, u32[]{:S(2)}, u32[]{:S(2)}) collective-permute-start(f32[2,256,256]{2,1,0:T(8,128)} %shard_map.79), channel_id=1, source_target_pairs={{0,6},{2,0},{4,2},{6,4},{1,7},{3,1},{5,3},{7,5},{8,14},{10,8},{12,... | collective-permute-start | bytes 1572872 | tf_op jit(solution)/shard_map/ppermute | solution.py:208
  91.8 2.2 %shard_map.84 = (f32[256,256]{1,0:T(8,128)S(1)}, f32[256,256]{1,0:T(8,128)S(1)}) custom-call(s32[3]{0:T(128)S(1)} %pad_add_fusion.1.cols_ref, bf16[256,512]{1,0:T(8,128)(2,1)S(1)} %copy-done.1, bf16[512,4096]{1,0:T(8,128)(2,1)} %weight_ref.15, f32[2,256,256]{2,1,0:T(8,128)S(1)} %collective-permute-done.6.left_ref, ...), custom_call_target="tpu_custom_call" | custom-call | flops 134217728 | bytes 1048576 | tf_op jit(solution)/shard_map/pallas_call | solution.py:179
  94.0 7.9 %collective-permute-start.9 = (f32[256,256]{1,0:T(8,128)S(1)}, f32[256,256]{1,0:T(8,128)S(1)}, u32[]{:S(2)}, u32[]{:S(2)}) collective-permute-start(f32[256,256]{1,0:T(8,128)S(1)} %get-tuple-element.32), channel_id=1, source_target_pairs={{0,1},{1,0},{2,3},{3,2},{4,5},{5,4},{6,7},{7,6},{8,9},{9,8},{10,11... | collective-permute-start | bytes 786440 | tf_op jit(solution)/shard_map/ppermute | solution.py:208
  102.0 2.7 %shard_map.80 = (f32[256,256]{1,0:T(8,128)S(1)}, f32[256,256]{1,0:T(8,128)S(1)}) custom-call(s32[3]{0:T(128)S(1)} %pad_add_fusion.cols_ref, bf16[256,512]{1,0:T(8,128)(2,1)S(1)} %copy-done.1, bf16[512,4096]{1,0:T(8,128)(2,1)} %weight_ref.15, f32[2,256,256]{2,1,0:T(8,128)S(1)} %collective-permute-done.1.left_ref, f32[2,256,256]{2,1,0:T(8,128)} %collective-permute-done.3.right_ref), custom_call_target="tpu_custom_call" | custom-call | flops 134217728 | bytes 1048576 | tf_op jit(solution)/shard_map/pallas_call | solution.py:179
  104.7 6.4 %collective-permute-start.4 = (f32[256,256]{1,0:T(8,128)S(1)}, f32[256,256]{1,0:T(8,128)S(1)}, u32[]{:S(2)}, u32[]{:S(2)}) collective-permute-start(f32[256,256]{1,0:T(8,128)S(1)} %get-tuple-element.28), channel_id=1, source_target_pairs={{0,1},{1,0},{2,3},{3,2},{4,5},{5,4},{6,7},{7,6},{8,9},{9,8},{10,11... | collective-permute-start | bytes 786440 | tf_op jit(solution)/shard_map/ppermute | solution.py:208
  111.1 35.4 %collective-permute-done.9 = f32[256,256]{1,0:T(8,128)S(1)} collective-permute-done((f32[256,256]{1,0:T(8,128)S(1)}, f32[256,256]{1,0:T(8,128)S(1)}, u32[]{:S(2)}, u32[]{:S(2)}) %collective-permute-start.9) | collective-permute-done | bytes 262176 | tf_op jit(solution)/shard_map/ppermute | solution.py:208
  146.5 5.6 %collective-permute-done.4 = f32[256,256]{1,0:T(8,128)S(1)} collective-permute-done((f32[256,256]{1,0:T(8,128)S(1)}, f32[256,256]{1,0:T(8,128)S(1)}, u32[]{:S(2)}, u32[]{:S(2)}) %collective-permute-start.4) | collective-permute-done | bytes 262176 | tf_op jit(solution)/shard_map/ppermute | solution.py:208
  152.2 0.7 pad_maximum_fusion
  (23 shorter events, 0.4 us)
Async XLA Ops:
  3.0 27.1 %all-to-all-start = ((f32[64,1,128]{2,1,0:T(1,128)}), f32[64,1,128]{2,1,0:T(1,128)S(1)}, u32[]{:S(2)}, u32[]{:S(2)}) async-start(f32[64,1,128]{2,1,0:T(1,128)} %bitcast.17), calls=%async_computation | async-start | bytes 65536 | tf_op jit(solution)/shard_map/all_to_all | solution.py:224
  30.8 17.0 %all-to-all-start.1 = ((f32[64,1,128]{2,1,0:T(1,128)}), f32[64,1,128]{2,1,0:T(1,128)S(1)}, u32[]{:S(2)}, u32[]{:S(2)}) async-start(f32[64,1,128]{2,1,0:T(1,128)} %bitcast.9), calls=%async_computation.1 | async-start | bytes 65536 | tf_op jit(solution)/shard_map/all_to_all | solution.py:226
  47.8 0.6 copy-start.2
  51.1 0.9 copy-start
  52.1 8.7 %copy-start.1 = (bf16[256,512]{1,0:T(8,128)(2,1)S(1)}, bf16[256,512]{1,0:T(8,128)(2,1)}, u32[]{:S(2)}) copy-start(bf16[256,512]{1,0:T(8,128)(2,1)} %shard_map.76.gated_ref) | copy-start | bytes 786436
  54.2 15.2 %collective-permute-start.5 = (f32[256,256]{1,0:T(8,128)S(1)}, f32[256,256]{1,0:T(8,128)S(1)}, u32[]{:S(2)}, u32[]{:S(2)}) collective-permute-start(f32[256,256]{1,0:T(8,128)S(1)} %get-tuple-element.29), channel_id=1, source_target_pairs={{0,2},{2,4},{4,6},{6,0},{1,3},{3,5},{5,7},{7,1},{8,10},{10,12},{12... | collective-permute-start | bytes 786440 | tf_op jit(solution)/shard_map/ppermute | solution.py:208
  57.3 16.1 %collective-permute-start.7 = (f32[256,256]{1,0:T(8,128)S(1)}, f32[256,256]{1,0:T(8,128)S(1)}, u32[]{:S(2)}, u32[]{:S(2)}) collective-permute-start(f32[256,256]{1,0:T(8,128)S(1)} %get-tuple-element.30), channel_id=1, source_target_pairs={{0,6},{2,0},{4,2},{6,4},{1,7},{3,1},{5,3},{7,5},{8,14},{10,8},{12,... | collective-permute-start | bytes 786440 | tf_op jit(solution)/shard_map/ppermute | solution.py:208
  62.8 17.3 %collective-permute-start = (f32[256,256]{1,0:T(8,128)S(1)}, f32[256,256]{1,0:T(8,128)S(1)}, u32[]{:S(2)}, u32[]{:S(2)}) collective-permute-start(f32[256,256]{1,0:T(8,128)S(1)} %get-tuple-element.25), channel_id=1, source_target_pairs={{0,2},{2,4},{4,6},{6,0},{1,3},{3,5},{5,7},{7,1},{8,10},{10,12},{12... | collective-permute-start | bytes 786440 | tf_op jit(solution)/shard_map/ppermute | solution.py:208
  64.8 19.4 %collective-permute-start.2 = (f32[256,256]{1,0:T(8,128)S(1)}, f32[256,256]{1,0:T(8,128)S(1)}, u32[]{:S(2)}, u32[]{:S(2)}) collective-permute-start(f32[256,256]{1,0:T(8,128)S(1)} %get-tuple-element.26), channel_id=1, source_target_pairs={{0,6},{2,0},{4,2},{6,4},{1,7},{3,1},{5,3},{7,5},{8,14},{10,8},{12,... | collective-permute-start | bytes 786440 | tf_op jit(solution)/shard_map/ppermute | solution.py:208
  71.5 20.3 %collective-permute-start.6 = (f32[2,256,256]{2,1,0:T(8,128)S(1)}, f32[2,256,256]{2,1,0:T(8,128)S(1)}, u32[]{:S(2)}, u32[]{:S(2)}) collective-permute-start(f32[2,256,256]{2,1,0:T(8,128)S(1)} %shard_map.82), channel_id=1, source_target_pairs={{0,2},{2,4},{4,6},{6,0},{1,3},{3,5},{5,7},{7,1},{8,10},{10,12},{12... | collective-permute-start | bytes 1572872 | tf_op jit(solution)/shard_map/ppermute | solution.py:208
  75.5 16.3 %collective-permute-start.8 = (f32[2,256,256]{2,1,0:T(8,128)S(1)}, f32[2,256,256]{2,1,0:T(8,128)S(1)}, u32[]{:S(2)}, u32[]{:S(2)}) collective-permute-start(f32[2,256,256]{2,1,0:T(8,128)S(1)} %shard_map.83), channel_id=1, source_target_pairs={{0,6},{2,0},{4,2},{6,4},{1,7},{3,1},{5,3},{7,5},{8,14},{10,8},{12,... | collective-permute-start | bytes 1572872 | tf_op jit(solution)/shard_map/ppermute | solution.py:208
  82.2 19.8 %collective-permute-start.1 = (f32[2,256,256]{2,1,0:T(8,128)S(1)}, f32[2,256,256]{2,1,0:T(8,128)S(1)}, u32[]{:S(2)}, u32[]{:S(2)}) collective-permute-start(f32[2,256,256]{2,1,0:T(8,128)S(1)} %shard_map.78), channel_id=1, source_target_pairs={{0,2},{2,4},{4,6},{6,0},{1,3},{3,5},{5,7},{7,1},{8,10},{10,12},{12... | collective-permute-start | bytes 1572872 | tf_op jit(solution)/shard_map/ppermute | solution.py:208
  87.0 15.0 %collective-permute-start.3 = (f32[2,256,256]{2,1,0:T(8,128)}, f32[2,256,256]{2,1,0:T(8,128)}, u32[]{:S(2)}, u32[]{:S(2)}) collective-permute-start(f32[2,256,256]{2,1,0:T(8,128)} %shard_map.79), channel_id=1, source_target_pairs={{0,6},{2,0},{4,2},{6,4},{1,7},{3,1},{5,3},{7,5},{8,14},{10,8},{12,... | collective-permute-start | bytes 1572872 | tf_op jit(solution)/shard_map/ppermute | solution.py:208
  94.0 52.5 %collective-permute-start.9 = (f32[256,256]{1,0:T(8,128)S(1)}, f32[256,256]{1,0:T(8,128)S(1)}, u32[]{:S(2)}, u32[]{:S(2)}) collective-permute-start(f32[256,256]{1,0:T(8,128)S(1)} %get-tuple-element.32), channel_id=1, source_target_pairs={{0,1},{1,0},{2,3},{3,2},{4,5},{5,4},{6,7},{7,6},{8,9},{9,8},{10,11... | collective-permute-start | bytes 786440 | tf_op jit(solution)/shard_map/ppermute | solution.py:208
  104.7 47.4 %collective-permute-start.4 = (f32[256,256]{1,0:T(8,128)S(1)}, f32[256,256]{1,0:T(8,128)S(1)}, u32[]{:S(2)}, u32[]{:S(2)}) collective-permute-start(f32[256,256]{1,0:T(8,128)S(1)} %get-tuple-element.28), channel_id=1, source_target_pairs={{0,1},{1,0},{2,3},{3,2},{4,5},{5,4},{6,7},{7,6},{8,9},{9,8},{10,11... | collective-permute-start | bytes 786440 | tf_op jit(solution)/shard_map/ppermute | solution.py:208

commit v2 on v1

--- a/solution.py
+++ b/solution.py
@@ -13,7 +13,8 @@
 SUBS = 8
 ALL_VMEM = 56 * 1024 * 1024
 MOST_VMEM = 52 * 1024 * 1024
-CHUNKS = 2
+GATE_VMEM = 56 * 1024 * 1024
+WIDTHS = (256, 256)
 SEQ_PARTS = (("y", 4), ("zl", 8), ("core", 2))
 CHAN_PARTS = (("x", 4), ("zh", 2))
 SEQ = tuple(name for name, _ in SEQ_PARTS)
@@ -117,7 +118,9 @@
         out_ref[rows, :] = y_ref[rows, :] + skip_ref[:, lanes] * x_ref[rows, :]
 
 
-def gate_kernel(q_ref, local_ref, rate_ref, coef_ref, enter_ref, out_ref, y_ref):
+def gate_kernel(cols_ref, q_ref, local_ref, rate_ref, coef_ref, enter_ref, weight_ref, *refs):
+    out_ref, far_ref, near_ref, y_ref, block_ref, sems = refs
+    fetches = start_fetches(cols_ref, weight_ref, block_ref, sems)
     tokens, chans = q_ref.shape
     modes = rate_ref.shape[0]
     run = tokens // SUBS
@@ -139,25 +142,34 @@
         rows = pl.ds(tile * tokens, tokens)
         value = q_ref[:, lanes].astype(F32) * (local_ref[rows, :] + y_ref[rows, :])
         out_ref[:, lanes] = value.astype(out_ref.dtype)
-
-
-def project_kernel(adds, joined, width, cols_ref, gated_ref, weight_ref, *refs):
-    terms, outs, (block_ref, sems) = refs[: len(adds)], refs[len(adds) : -2], refs[-2:]
-    fetches = start_fetches(cols_ref, width, weight_ref, block_ref, sems)
-    for half in range(2):
-        fetches[half].wait()
-        block = jnp.dot(gated_ref[...], block_ref[half], preferred_element_type=F32)
-        for which, term in zip(adds, terms):
-            if which == half:
-                block = block + term[...]
-        if joined:
-            outs[0][half] = block
-        else:
-            outs[half][...] = block
-
-
-def own_kernel(width, cols_ref, gated_ref, weight_ref, left_ref, right_ref, keep_ref, send_ref, block_ref, sems):
-    fetches = start_fetches(cols_ref, width, weight_ref, block_ref, sems)
+    multiply(fetches, out_ref, block_ref, (far_ref, near_ref))
+
+
+def start_fetches(cols_ref, weight_ref, block_ref, sems):
+    fetches = []
+    for i in range(block_ref.shape[0]):
+        lanes = pl.ds(pl.multiple_of(cols_ref[i] * LANES, LANES), block_ref.shape[2])
+        fetches.append(pltpu.make_async_copy(weight_ref.at[:, lanes], block_ref.at[i], sems.at[i]))
+        fetches[-1].start()
+    return fetches
+
+
+def multiply(fetches, gated_ref, block_ref, outs, adds=()):
+    for i, fetch in enumerate(fetches):
+        fetch.wait()
+        block = jnp.dot(gated_ref[...], block_ref[i], preferred_element_type=F32)
+        for add in adds:
+            block = block + add[i]
+        outs[i // 2][i % 2] = block
+
+
+def project_kernel(count, cols_ref, gated_ref, weight_ref, *refs):
+    adds, outs, (block_ref, sems) = refs[: -2 - count], refs[-2 - count : -2], refs[-2:]
+    multiply(start_fetches(cols_ref, weight_ref, block_ref, sems), gated_ref, block_ref, outs, adds)
+
+
+def own_kernel(cols_ref, gated_ref, weight_ref, left_ref, right_ref, keep_ref, send_ref, block_ref, sems):
+    fetches = start_fetches(cols_ref, weight_ref, block_ref, sems)
     mine = cols_ref[2]
     for half, at, out in ((1, 1 - mine, send_ref), (0, mine, keep_ref)):
         fetches[half].wait()
@@ -165,42 +177,14 @@
         out[...] = block + left_ref[at] + right_ref[at]
 
 
-def start_fetches(cols_ref, width, weight_ref, block_ref, sems):
-    fetches = []
-    for half in range(2):
-        lanes = pl.ds(pl.multiple_of(cols_ref[half] * width, LANES), width)
-        fetches.append(pltpu.make_async_copy(weight_ref.at[:, lanes], block_ref.at[half], sems.at[half]))
-        fetches[-1].start()
-    return fetches
-
-
-def project_call(kernel, shapes, width, cols, gated, weight, terms):
+def fetched(weight, blocks, width):
+    return [pltpu.VMEM((blocks, weight.shape[0], width), weight.dtype), pltpu.SemaphoreType.DMA((blocks,))]
+
+
+def project_call(kernel, shapes, blocks, width, cols, gated, weight, terms):
     vmem = pl.BlockSpec(memory_space=pltpu.VMEM)
-    return pl.pallas_call(
-        kernel,
-        in_specs=[pl.BlockSpec(memory_space=pltpu.SMEM), vmem, pl.BlockSpec(memory_space=pl.ANY)] + [vmem] * len(terms),
-        out_specs=[vmem] * len(shapes),
-        out_shape=shapes,
-        scratch_shapes=[pltpu.VMEM((2, weight.shape[0], width), weight.dtype), pltpu.SemaphoreType.DMA((2,))],
-        compiler_params=pltpu.CompilerParams(vmem_limit_bytes=MOST_VMEM),
-        cost_estimate=pl.CostEstimate(flops=1 << 27, bytes_accessed=1 << 20, transcendentals=0),
-    )(cols, gated, weight, *terms)
-
-
-def project(gated, weight, cols, width, adds=(), terms=(), joined=False):
-    tokens = gated.shape[0]
-    if joined:
-        shapes = (jax.ShapeDtypeStruct((2, tokens, width), F32),)
-    else:
-        shapes = (jax.ShapeDtypeStruct((tokens, width), F32),) * 2
-    outs = project_call(functools.partial(project_kernel, adds, joined, width), shapes, width, cols, gated, weight, terms)
-    return outs[0] if joined else outs
-
-
-def project_own(gated, weight, cols, width, z_index, terms):
-    cols = jnp.concatenate([cols, z_index.astype(jnp.int32)[None]])
-    shapes = (jax.ShapeDtypeStruct((gated.shape[0], width), F32),) * 2
-    return project_call(functools.partial(own_kernel, width), shapes, width, cols, gated, weight, terms)
+    specs = [pl.BlockSpec(memory_space=pltpu.SMEM), vmem, pl.BlockSpec(memory_space=pl.ANY)] + [vmem] * len(terms)
+    return whole_call(kernel, shapes, fetched(weight, blocks, width), MOST_VMEM, (cols, gated, weight, *terms), specs)
 
 
 def shift(value, axis, by):
@@ -248,41 +232,53 @@
     scratch = [pltpu.VMEM(stacked.shape, F32)]
     local = whole_call(local_kernel, stacked, scratch, ALL_VMEM, (mixed, rate, coef, ends, skip_gain[None, :]))
     enter = entering_states(state, fade)
-    gated = jax.ShapeDtypeStruct((tokens, chans), queries.dtype)
-    gated = whole_call(gate_kernel, gated, scratch, ALL_VMEM, (queries, local, rate, coef, enter))
-
     x_size, x_index = lax.axis_size("x"), lax.axis_index("x")
-    z_size, z_index = lax.axis_size("zh"), lax.axis_index("zh")
+    z_size, z_index = lax.axis_size("zh"), lax.axis_index("zh").astype(jnp.int32)
     features = out_weight.shape[1] // (x_size * z_size)
-    width = features // CHUNKS
-
-    def cols(x_by, first, chunk):
-        start = ((x_index + x_by) % x_size) * z_size
-        return ((start + jnp.stack([first, 1 - first])) * CHUNKS + chunk).astype(jnp.int32)
-
-    zero = jnp.int32(0)
-    outs, summed, kept, swapped = [], [], [], []
-    for chunk in range(CHUNKS + 2):
-        if chunk < CHUNKS:
-            behind = summed[chunk - 2 :] + kept[chunk - 3 :] if chunk >= 2 else []
-            source, *_ = lax.optimization_barrier((gated, *behind))
-            far = project(source, out_weight, cols(2, zero, chunk), width)
-            summed.append((shift(far[0], "x", 1), shift(far[1], "x", -1)))
-        if 1 <= chunk <= CHUNKS:
-            at = chunk - 1
-            from_left, from_right = summed[at]
-            source, *_ = lax.optimization_barrier((gated, *swapped[at - 3 :])) if at >= 3 else (gated,)
-            right = project(source, out_weight, cols(1, zero, at), width, (0,), (from_left,), True)
-            left = project(source, out_weight, cols(-1, zero, at), width, (1,), (from_right,), True)
-            summed[at] = (right, left)
-        if chunk >= 2:
-            at = chunk - 2
-            right, left = summed[at]
-            terms = (shift(right, "x", 1), shift(left, "x", -1))
-            keep, send = project_own(gated, out_weight, cols(0, z_index, at), width, z_index, terms)
-            kept.append(send)
-            swapped.append(shift(send, "zh", 1))
-            outs.append(keep + swapped[at])
+
+    def cols(x_bys, chunk, first=jnp.int32(0)):
+        lanes = []
+        for x_by in x_bys:
+            start = ((x_index + x_by) % x_size) * z_size
+            lanes += [(start + z) * features + sum(WIDTHS[:chunk]) for z in (first, 1 - first)]
+        return (jnp.stack(lanes) // LANES).astype(jnp.int32)
+
+    def pair(chunk):
+        return jax.ShapeDtypeStruct((2, tokens, WIDTHS[chunk]), F32)
+
+    vmem, anywhere = pl.BlockSpec(memory_space=pltpu.VMEM), pl.BlockSpec(memory_space=pl.ANY)
+    gated, far, near = whole_call(
+        gate_kernel,
+        (jax.ShapeDtypeStruct((tokens, chans), queries.dtype), pair(0), pair(0)),
+        scratch + fetched(out_weight, 4, WIDTHS[0]),
+        GATE_VMEM,
+        (cols((2, -1), 0), queries, local, rate, coef, enter, out_weight),
+        [pl.BlockSpec(memory_space=pltpu.SMEM)] + [vmem] * 5 + [anywhere],
+    )
+    ways = [1 if chunk % 2 == 0 else -1 for chunk in range(len(WIDTHS))]
+    firsts = []
+    for chunk, way in enumerate(ways):
+        if chunk:
+            kernel = functools.partial(project_kernel, 2)
+            at = cols((2, -way), chunk)
+            far, near = project_call(
+                kernel, (pair(chunk), pair(chunk)), 4, WIDTHS[chunk], at, gated, out_weight, ()
+            )
+        firsts.append((shift(far, "x", way), near))
+    seconds = []
+    for chunk, way in enumerate(ways):
+        passed, near = firsts[chunk]
+        kernel = functools.partial(project_kernel, 1)
+        (both,) = project_call(
+            kernel, (pair(chunk),), 2, WIDTHS[chunk], cols((way,), chunk), gated, out_weight, (passed,)
+        )
+        seconds.append((shift(both, "x", way), shift(near, "x", -way)))
+    outs = []
+    for chunk, terms in enumerate(seconds):
+        at = jnp.concatenate([cols((0,), chunk, z_index), z_index[None]])
+        block = jax.ShapeDtypeStruct((tokens, WIDTHS[chunk]), F32)
+        keep, send = project_call(own_kernel, (block, block), 2, WIDTHS[chunk], at, gated, out_weight, terms)
+        outs.append(keep + shift(send, "zh", 1))
     return jnp.concatenate(outs, axis=1).astype(jnp.bfloat16)
 
 

time: 154 us -> 148 us (0.961)
  the two profiles are of different devices: /device:TPU:33 before, /device:TPU:39 now
where the time goes in v2:
time: 148 us; the launch traced here: 147 us
  waiting for transfers between devices  64.7 us (44%)
  starting transfers between devices  54.4 us (37%)
  Pallas kernels  23.5 us (16%)
  local copies, waits for them, and re-layouts  2.26 us (2%)
  other arithmetic  1.92 us (1%)
    ppermute x8, waiting for transfers between devices, shift(): lax.ppermute(value, axis, [(i, (i + by) % size) for i in range(size)])  48.1 us
    ppermute x8, starting transfers between devices, shift(): lax.ppermute(value, axis, [(i, (i + by) % size) for i in range(size)])  32.2 us
    pallas_call x9, Pallas kernels, whole_call(): pl.pallas_call(kernel, in_specs=in_specs or [pl.BlockSpec(memory_space=pl...  23.5 us
    all_to_all x1, starting transfers between devices, entering_states(): state = lax.all_to_all(state, SEQ, 0, 0, tiled=True)  16.1 us
    all_to_all x1, waiting for transfers between devices, entering_states(): state = lax.all_to_all(state, SEQ, 0, 0, tiled=True)  10.2 us
    all_to_all x1, waiting for transfers between devices, entering_states(): return lax.all_to_all(enter, SEQ, 0, 0, tiled=True)  6.4 us
    all_to_all x1, starting transfers between devices, entering_states(): return lax.all_to_all(enter, SEQ, 0, 0, tiled=True)  6.04 us
  transfers between devices with their start and end apart: 10, of which 7 were waited for; matrix products, arithmetic and copies ran while one was open for 1% of the time, Pallas kernels for 11%

profile of v2, /device:TPU:39, one launch (start us, length us, event | category | flops | bytes accessed | tf_op | source)
XLA Modules:
  0.0 147.0 jit_solution(13390195925826322971)
XLA Ops:
  0.0 3.0 %shard_map.73 = (f32[16,512]{1,0:T(8,128)}, f32[16,512]{1,0:T(8,128)}, f32[16,8,512]{2,1,0:T(8,128)}, f32[64,128]{1,0:T(8,128)}, f32[64,128]{1,0:T(8,128)}, /*index=5*/f32[1024,128]{1,0:T(8,128)}) custom-call(bf16[256,512]{1,0:T(8,128)(2,1)} %refs_0_.1, bf16[256,512]{1,0:T(8,128)(2,1)} %refs_1_.1, f32[16,512]{1,0:T(8,128)} %bitcast.30, f32[16,512]{1,0:T(8,128)} %bitcast.31), custom_call_target="tpu_custom_call" | custom-call | flops 16777216 | bytes 2097152 | tf_op jit(solution)/shard_map/pallas_call | solution.py:31
  3.0 16.1 %all-to-all-start = ((f32[64,1,128]{2,1,0:T(1,128)}), f32[64,1,128]{2,1,0:T(1,128)S(1)}, u32[]{:S(2)}, u32[]{:S(2)}) async-start(f32[64,1,128]{2,1,0:T(1,128)} %bitcast.32), calls=%async_computation | async-start | bytes 65536 | tf_op jit(solution)/shard_map/all_to_all | solution.py:208
  19.1 0.7 constant_dynamic-slice_fusion.fade_ref
  19.8 10.2 %all-to-all-done = f32[64,1,128]{2,1,0:T(1,128)S(1)} async-done(((f32[64,1,128]{2,1,0:T(1,128)}), f32[64,1,128]{2,1,0:T(1,128)S(1)}, u32[]{:S(2)}, u32[]{:S(2)}) %all-to-all-start) | async-done | bytes 32800 | tf_op jit(solution)/shard_map/all_to_all | solution.py:208
  30.0 0.7 shard_map.75
  30.8 6.0 %all-to-all-start.1 = ((f32[64,1,128]{2,1,0:T(1,128)}), f32[64,1,128]{2,1,0:T(1,128)S(1)}, u32[]{:S(2)}, u32[]{:S(2)}) async-start(f32[64,1,128]{2,1,0:T(1,128)} %bitcast.14), calls=%async_computation.1 | async-start | bytes 65536 | tf_op jit(solution)/shard_map/all_to_all | solution.py:210
  36.8 4.0 %shard_map.74.local_ref = f32[1024,128]{1,0:T(8,128)} custom-call(f32[1024,128]{1,0:T(8,128)} %get-tuple-element.20.x_ref, f32[16,512]{1,0:T(8,128)} %get-tuple-element.21.rate_ref, f32[16,512]{1,0:T(8,128)} %get-tuple-element.22.coef_ref, f32[16,8,512]{2,1,0:T(8,128)} %get-tuple-element.23.ends_ref, f32[1,512]{1,0:T(1,128)} %bitcast.33), custom_call_target="tpu_custom_call" | custom-call | flops 16777216 | bytes 2097152 | tf_op jit(solution)/shard_map/pallas_call | solution.py:31
  40.8 0.6 and_select_fusion.4.cols_ref
  41.4 6.4 %all-to-all-done.1 = f32[64,1,128]{2,1,0:T(1,128)S(1)} async-done(((f32[64,1,128]{2,1,0:T(1,128)}), f32[64,1,128]{2,1,0:T(1,128)S(1)}, u32[]{:S(2)}, u32[]{:S(2)}) %all-to-all-start.1) | async-done | bytes 32800 | tf_op jit(solution)/shard_map/all_to_all | solution.py:210
  47.8 0.6 copy-done.3
  48.4 4.1 %shard_map.76 = (bf16[256,512]{1,0:T(8,128)(2,1)}, f32[2,256,256]{2,1,0:T(8,128)}, f32[2,256,256]{2,1,0:T(8,128)}) custom-call(s32[4]{0:T(128)} %and_select_fusion.4.cols_ref, bf16[256,512]{1,0:T(8,128)(2,1)} %q_ref.1, f32[1024,128]{1,0:T(8,128)} %shard_map.74.local_ref, f32[16,512]{1,0:T(8,128)} %get-tuple-element.21.rate_ref, ...), custom_call_target="tpu_custom_call" | custom-call | flops 16777216 | bytes 2097152 | tf_op jit(solution)/shard_map/pallas_call | solution.py:31
  52.5 2.1 %collective-permute-start = (f32[2,256,256]{2,1,0:T(8,128)}, f32[2,256,256]{2,1,0:T(8,128)S(1)}, u32[]{:S(2)}, u32[]{:S(2)}) collective-permute-start(f32[2,256,256]{2,1,0:T(8,128)} %get-tuple-element.27), channel_id=1, source_target_pairs={{0,2},{2,4},{4,6},{6,0},{1,3},{3,5},{5,7},{7,1},{8,10},{10,12},{12... | collective-permute-start | bytes 1572872 | tf_op jit(solution)/shard_map/ppermute | solution.py:192
  54.7 0.9 copy-done
  55.7 3.2 %shard_map.79 = (f32[2,256,256]{2,1,0:T(8,128)}, f32[2,256,256]{2,1,0:T(8,128)S(1)}) custom-call(s32[4]{0:T(128)S(1)} %and_select_fusion.cols_ref, bf16[256,512]{1,0:T(8,128)(2,1)S(1)} %copy-done, bf16[512,4096]{1,0:T(8,128)(2,1)} %weight_ref.11), custom_call_target="tpu_custom_call" | custom-call | flops 16777216 | bytes 2097152 | tf_op jit(solution)/shard_map/pallas_call | solution.py:31
  58.9 3.2 %collective-permute-start.4 = (f32[2,256,256]{2,1,0:T(8,128)}, f32[2,256,256]{2,1,0:T(8,128)S(1)}, u32[]{:S(2)}, u32[]{:S(2)}) collective-permute-start(f32[2,256,256]{2,1,0:T(8,128)} %get-tuple-element.31), channel_id=1, source_target_pairs={{0,6},{2,0},{4,2},{6,4},{1,7},{3,1},{5,3},{7,5},{8,14},{10,8},{12,... | collective-permute-start | bytes 1572872 | tf_op jit(solution)/shard_map/ppermute | solution.py:192
  62.1 0.1 and_select_fusion.3.cols_ref
  62.2 2.4 %collective-permute-start.2 = (f32[2,256,256]{2,1,0:T(8,128)}, f32[2,256,256]{2,1,0:T(8,128)S(1)}, u32[]{:S(2)}, u32[]{:S(2)}) collective-permute-start(f32[2,256,256]{2,1,0:T(8,128)} %get-tuple-element.28), channel_id=1, source_target_pairs={{0,6},{2,0},{4,2},{6,4},{1,7},{3,1},{5,3},{7,5},{8,14},{10,8},{12,... | collective-permute-start | bytes 1572872 | tf_op jit(solution)/shard_map/ppermute | solution.py:192
  64.6 2.8 %collective-permute-done.refs_0_ = f32[2,256,256]{2,1,0:T(8,128)S(1)} collective-permute-done((f32[2,256,256]{2,1,0:T(8,128)}, f32[2,256,256]{2,1,0:T(8,128)S(1)}, u32[]{:S(2)}, u32[]{:S(2)}) %collective-permute-start) | collective-permute-done | bytes 524320 | tf_op jit(solution)/shard_map/ppermute | solution.py:192
  67.4 2.1 %shard_map.77 = f32[2,256,256]{2,1,0:T(8,128)S(1)} custom-call(s32[2]{0:T(128)S(1)} %and_select_fusion.3.cols_ref, bf16[256,512]{1,0:T(8,128)(2,1)S(1)} %copy-done, bf16[512,4096]{1,0:T(8,128)(2,1)} %weight_ref.11, f32[2,256,256]{2,1,0:T(8,128)S(1)} %collective-permute-done.refs_0_), custom_call_target="tpu_custom_call" | custom-call | flops 16777216 | bytes 2097152 | tf_op jit(solution)/shard_map/pallas_call | solution.py:31
  69.5 3.3 %collective-permute-start.1 = (f32[2,256,256]{2,1,0:T(8,128)S(1)}, f32[2,256,256]{2,1,0:T(8,128)S(1)}, u32[]{:S(2)}, u32[]{:S(2)}) collective-permute-start(f32[2,256,256]{2,1,0:T(8,128)S(1)} %shard_map.77), channel_id=1, source_target_pairs={{0,2},{2,4},{4,6},{6,0},{1,3},{3,5},{5,7},{7,1},{8,10},{10,12},{12... | collective-permute-start | bytes 1572872 | tf_op jit(solution)/shard_map/ppermute | solution.py:192
  72.9 1.9 %collective-permute-start.6 = (f32[2,256,256]{2,1,0:T(8,128)}, f32[2,256,256]{2,1,0:T(8,128)S(1)}, u32[]{:S(2)}, u32[]{:S(2)}) collective-permute-start(f32[2,256,256]{2,1,0:T(8,128)} %copy-done.2), channel_id=1, source_target_pairs={{0,2},{2,4},{4,6},{6,0},{1,3},{3,5},{5,7},{7,1},{8,10},{10,12},{12... | collective-permute-start | bytes 1572872 | tf_op jit(solution)/shard_map/ppermute | solution.py:192
  74.8 2.1 %shard_map.80 = f32[2,256,256]{2,1,0:T(8,128)S(1)} custom-call(s32[2]{0:T(128)S(1)} %and_select_fusion.1.cols_ref, bf16[256,512]{1,0:T(8,128)(2,1)S(1)} %copy-done.1, bf16[512,4096]{1,0:T(8,128)(2,1)} %weight_ref.11, f32[2,256,256]{2,1,0:T(8,128)S(1)} %collective-permute-done.4.refs_0_), custom_call_target="tpu_custom_call" | custom-call | flops 16777216 | bytes 2097152 | tf_op jit(solution)/shard_map/pallas_call | solution.py:31
  76.9 3.4 %collective-permute-start.5 = (f32[2,256,256]{2,1,0:T(8,128)S(1)}, f32[2,256,256]{2,1,0:T(8,128)S(1)}, u32[]{:S(2)}, u32[]{:S(2)}) collective-permute-start(f32[2,256,256]{2,1,0:T(8,128)S(1)} %shard_map.80), channel_id=1, source_target_pairs={{0,6},{2,0},{4,2},{6,4},{1,7},{3,1},{5,3},{7,5},{8,14},{10,8},{12,... | collective-permute-start | bytes 1572872 | tf_op jit(solution)/shard_map/ppermute | solution.py:192
  80.5 5.5 %collective-permute-done.2.right_ref = f32[2,256,256]{2,1,0:T(8,128)S(1)} collective-permute-done((f32[2,256,256]{2,1,0:T(8,128)}, f32[2,256,256]{2,1,0:T(8,128)S(1)}, u32[]{:S(2)}, u32[]{:S(2)}) %collective-permute-start.2) | collective-permute-done | bytes 524320 | tf_op jit(solution)/shard_map/ppermute | solution.py:192
  85.9 2.2 %shard_map.78 = (f32[256,256]{1,0:T(8,128)S(1)}, f32[256,256]{1,0:T(8,128)S(1)}) custom-call(s32[3]{0:T(128)S(1)} %pad_add_fusion.1.cols_ref, bf16[256,512]{1,0:T(8,128)(2,1)S(1)} %copy-done.1, bf16[512,4096]{1,0:T(8,128)(2,1)} %weight_ref.11, f32[2,256,256]{2,1,0:T(8,128)S(1)} %collective-permute-done.1.left_ref, ...), custom_call_target="tpu_custom_call" | custom-call | flops 16777216 | bytes 2097152 | tf_op jit(solution)/shard_map/pallas_call | solution.py:31
  88.1 7.9 %collective-permute-start.3 = (f32[256,256]{1,0:T(8,128)S(1)}, f32[256,256]{1,0:T(8,128)S(1)}, u32[]{:S(2)}, u32[]{:S(2)}) collective-permute-start(f32[256,256]{1,0:T(8,128)S(1)} %get-tuple-element.30), channel_id=1, source_target_pairs={{0,1},{1,0},{2,3},{3,2},{4,5},{5,4},{6,7},{7,6},{8,9},{9,8},{10,11... | collective-permute-start | bytes 786440 | tf_op jit(solution)/shard_map/ppermute | solution.py:192
  96.2 0.9 collective-permute-done.5.left_ref
  97.2 2.2 %shard_map.81 = (f32[256,256]{1,0:T(8,128)S(1)}, f32[256,256]{1,0:T(8,128)S(1)}) custom-call(s32[3]{0:T(128)S(1)} %pad_add_fusion.5.cols_ref, bf16[256,512]{1,0:T(8,128)(2,1)S(1)} %copy-done.1, bf16[512,4096]{1,0:T(8,128)(2,1)} %weight_ref.11, f32[2,256,256]{2,1,0:T(8,128)S(1)} %collective-permute-done.5.left_ref, ...), custom_call_target="tpu_custom_call" | custom-call | flops 16777216 | bytes 2097152 | tf_op jit(solution)/shard_map/pallas_call | solution.py:31
  99.3 7.9 %collective-permute-start.7 = (f32[256,256]{1,0:T(8,128)S(1)}, f32[256,256]{1,0:T(8,128)S(1)}, u32[]{:S(2)}, u32[]{:S(2)}) collective-permute-start(f32[256,256]{1,0:T(8,128)S(1)} %get-tuple-element.34), channel_id=1, source_target_pairs={{0,1},{1,0},{2,3},{3,2},{4,5},{5,4},{6,7},{7,6},{8,9},{9,8},{10,11... | collective-permute-start | bytes 786440 | tf_op jit(solution)/shard_map/ppermute | solution.py:192
  107.3 33.4 %collective-permute-done.3 = f32[256,256]{1,0:T(8,128)S(1)} collective-permute-done((f32[256,256]{1,0:T(8,128)S(1)}, f32[256,256]{1,0:T(8,128)S(1)}, u32[]{:S(2)}, u32[]{:S(2)}) %collective-permute-start.3) | collective-permute-done | bytes 262176 | tf_op jit(solution)/shard_map/ppermute | solution.py:192
  140.7 5.6 %collective-permute-done.7 = f32[256,256]{1,0:T(8,128)S(1)} collective-permute-done((f32[256,256]{1,0:T(8,128)S(1)}, f32[256,256]{1,0:T(8,128)S(1)}, u32[]{:S(2)}, u32[]{:S(2)}) %collective-permute-start.7) | collective-permute-done | bytes 262176 | tf_op jit(solution)/shard_map/ppermute | solution.py:192
  146.3 0.7 pad_maximum_fusion
  (17 shorter events, 0.6 us)
Async XLA Ops:
  3.0 27.0 %all-to-all-start = ((f32[64,1,128]{2,1,0:T(1,128)}), f32[64,1,128]{2,1,0:T(1,128)S(1)}, u32[]{:S(2)}, u32[]{:S(2)}) async-start(f32[64,1,128]{2,1,0:T(1,128)} %bitcast.32), calls=%async_computation | async-start | bytes 65536 | tf_op jit(solution)/shard_map/all_to_all | solution.py:208
  30.8 17.0 %all-to-all-start.1 = ((f32[64,1,128]{2,1,0:T(1,128)}), f32[64,1,128]{2,1,0:T(1,128)S(1)}, u32[]{:S(2)}, u32[]{:S(2)}) async-start(f32[64,1,128]{2,1,0:T(1,128)} %bitcast.14), calls=%async_computation.1 | async-start | bytes 65536 | tf_op jit(solution)/shard_map/all_to_all | solution.py:210
  47.8 0.6 copy-start.3
  52.5 14.9 %collective-permute-start = (f32[2,256,256]{2,1,0:T(8,128)}, f32[2,256,256]{2,1,0:T(8,128)S(1)}, u32[]{:S(2)}, u32[]{:S(2)}) collective-permute-start(f32[2,256,256]{2,1,0:T(8,128)} %get-tuple-element.27), channel_id=1, source_target_pairs={{0,2},{2,4},{4,6},{6,0},{1,3},{3,5},{5,7},{7,1},{8,10},{10,12},{12... | collective-permute-start | bytes 1572872 | tf_op jit(solution)/shard_map/ppermute | solution.py:192
  54.7 1.0 copy-start
  55.7 19.2 %copy-start.1 = (bf16[256,512]{1,0:T(8,128)(2,1)S(1)}, bf16[256,512]{1,0:T(8,128)(2,1)}, u32[]{:S(2)}) copy-start(bf16[256,512]{1,0:T(8,128)(2,1)} %get-tuple-element.26.gated_ref) | copy-start | bytes 786436
  58.9 10.6 %copy-start.2 = (f32[2,256,256]{2,1,0:T(8,128)}, f32[2,256,256]{2,1,0:T(8,128)S(1)}, u32[]{:S(2)}) copy-start(f32[2,256,256]{2,1,0:T(8,128)S(1)} %get-tuple-element.32) | copy-start | bytes 1572868
  58.9 15.9 %collective-permute-start.4 = (f32[2,256,256]{2,1,0:T(8,128)}, f32[2,256,256]{2,1,0:T(8,128)S(1)}, u32[]{:S(2)}, u32[]{:S(2)}) collective-permute-start(f32[2,256,256]{2,1,0:T(8,128)} %get-tuple-element.31), channel_id=1, source_target_pairs={{0,6},{2,0},{4,2},{6,4},{1,7},{3,1},{5,3},{7,5},{8,14},{10,8},{12,... | collective-permute-start | bytes 1572872 | tf_op jit(solution)/shard_map/ppermute | solution.py:192
  62.2 23.8 %collective-permute-start.2 = (f32[2,256,256]{2,1,0:T(8,128)}, f32[2,256,256]{2,1,0:T(8,128)S(1)}, u32[]{:S(2)}, u32[]{:S(2)}) collective-permute-start(f32[2,256,256]{2,1,0:T(8,128)} %get-tuple-element.28), channel_id=1, source_target_pairs={{0,6},{2,0},{4,2},{6,4},{1,7},{3,1},{5,3},{7,5},{8,14},{10,8},{12,... | collective-permute-start | bytes 1572872 | tf_op jit(solution)/shard_map/ppermute | solution.py:192
  69.5 16.4 %collective-permute-start.1 = (f32[2,256,256]{2,1,0:T(8,128)S(1)}, f32[2,256,256]{2,1,0:T(8,128)S(1)}, u32[]{:S(2)}, u32[]{:S(2)}) collective-permute-start(f32[2,256,256]{2,1,0:T(8,128)S(1)} %shard_map.77), channel_id=1, source_target_pairs={{0,2},{2,4},{4,6},{6,0},{1,3},{3,5},{5,7},{7,1},{8,10},{10,12},{12... | collective-permute-start | bytes 1572872 | tf_op jit(solution)/shard_map/ppermute | solution.py:192
  72.9 23.3 %collective-permute-start.6 = (f32[2,256,256]{2,1,0:T(8,128)}, f32[2,256,256]{2,1,0:T(8,128)S(1)}, u32[]{:S(2)}, u32[]{:S(2)}) collective-permute-start(f32[2,256,256]{2,1,0:T(8,128)} %copy-done.2), channel_id=1, source_target_pairs={{0,2},{2,4},{4,6},{6,0},{1,3},{3,5},{5,7},{7,1},{8,10},{10,12},{12... | collective-permute-start | bytes 1572872 | tf_op jit(solution)/shard_map/ppermute | solution.py:192
  76.9 20.2 %collective-permute-start.5 = (f32[2,256,256]{2,1,0:T(8,128)S(1)}, f32[2,256,256]{2,1,0:T(8,128)S(1)}, u32[]{:S(2)}, u32[]{:S(2)}) collective-permute-start(f32[2,256,256]{2,1,0:T(8,128)S(1)} %shard_map.80), channel_id=1, source_target_pairs={{0,6},{2,0},{4,2},{6,4},{1,7},{3,1},{5,3},{7,5},{8,14},{10,8},{12,... | collective-permute-start | bytes 1572872 | tf_op jit(solution)/shard_map/ppermute | solution.py:192
  88.1 52.6 %collective-permute-start.3 = (f32[256,256]{1,0:T(8,128)S(1)}, f32[256,256]{1,0:T(8,128)S(1)}, u32[]{:S(2)}, u32[]{:S(2)}) collective-permute-start(f32[256,256]{1,0:T(8,128)S(1)} %get-tuple-element.30), channel_id=1, source_target_pairs={{0,1},{1,0},{2,3},{3,2},{4,5},{5,4},{6,7},{7,6},{8,9},{9,8},{10,11... | collective-permute-start | bytes 786440 | tf_op jit(solution)/shard_map/ppermute | solution.py:192
  99.3 47.0 %collective-permute-start.7 = (f32[256,256]{1,0:T(8,128)S(1)}, f32[256,256]{1,0:T(8,128)S(1)}, u32[]{:S(2)}, u32[]{:S(2)}) collective-permute-start(f32[256,256]{1,0:T(8,128)S(1)} %get-tuple-element.34), channel_id=1, source_target_pairs={{0,1},{1,0},{2,3},{3,2},{4,5},{5,4},{6,7},{7,6},{8,9},{9,8},{10,11... | collective-permute-start | bytes 786440 | tf_op jit(solution)/shard_map/ppermute | solution.py:192

commit v3 on v2

--- a/solution.py
+++ b/solution.py
@@ -52,7 +52,7 @@
 
 def state_kernel(length, *refs):
     hbm, refs = refs[:4], refs[4:]
-    rate_ref, coef_ref, ends_ref, state_ref, fade_ref, x_ref, *arrived, sems = refs
+    rate_ref, coef_ref, ends_ref, state_ref, x_ref, *arrived, sems = refs
     copies = [pltpu.make_async_copy(src, dst, sems.at[i]) for i, (src, dst) in enumerate(zip(hbm, arrived))]
     for copy in copies:
         copy.start()
@@ -80,9 +80,9 @@
         held = lax.fori_loop(0, run, body, held, unroll=8)
         for m in range(modes):
             ends_ref[m, :, lanes] = held[m]
-            row = m * (chans // LANES) + tile
-            state_ref[row : row + 1, :] = jnp.sum(held[m] * jnp.exp(-rates[m] * later), axis=0, keepdims=True)
-            fade_ref[row : row + 1, :] = jnp.exp(-rates[m][:1] * tokens)
+            state_ref[m : m + 1, lanes] = jnp.sum(
+                held[m] * jnp.exp(-rates[m] * later), axis=0, keepdims=True
+            )
 
 
 def local_kernel(x_ref, rate_ref, coef_ref, ends_ref, skip_ref, out_ref, y_ref):
@@ -131,7 +131,7 @@
         for m in range(modes):
             rate = spread_row(rate_ref, m, lanes)
             steps.append(jnp.exp(-rate))
-            weight = spread_row(coef_ref, m, lanes) * spread_row(enter_ref, m * (chans // LANES) + tile, slice(None))
+            weight = spread_row(coef_ref, m, lanes) * spread_row(enter_ref, m, lanes)
             held.append(weight * jnp.exp(-rate * place))
 
         def body(j, held, base=tile * tokens):
@@ -192,22 +192,27 @@
     return lax.ppermute(value, axis, [(i, (i + by) % size) for i in range(size)])
 
 
-def scan_kernel(state_ref, fade_ref, enter_ref):
-    count, total = fade_ref.shape[0], jnp.zeros(fade_ref.shape, F32)
-    for first in range(0, state_ref.shape[0], count):
-        enter_ref[first : first + count, :] = total
-        total = total * fade_ref[...] + state_ref[first : first + count, :]
-
-
-def entering_states(state, fade):
-    count, index = state.shape[0], jnp.int32(0)
-    for axis in SEQ:
-        count = count // lax.axis_size(axis)
-        index = index * lax.axis_size(axis) + lax.axis_index(axis)
-    fade = lax.dynamic_slice_in_dim(fade, index * count, count, 0)
-    state = lax.all_to_all(state, SEQ, 0, 0, tiled=True)
-    enter = whole_call(scan_kernel, jax.ShapeDtypeStruct(state.shape, F32), [], MOST_VMEM, (state, fade))
-    return lax.all_to_all(enter, SEQ, 0, 0, tiled=True)
+def entering_states(state, rate, tokens):
+    enter, total = jnp.zeros_like(state), state
+    offset, span = jnp.int32(0), 1
+    for axis in reversed(SEQ[1:]):
+        size, index = lax.axis_size(axis), lax.axis_index(axis)
+        by = 1
+        while by < size:
+            other = lax.ppermute(total, axis, [(i, i ^ by) for i in range(size)])
+            upper = (index & by) != 0
+            enter = enter + jnp.where(upper, jnp.exp(-rate * (offset * tokens).astype(F32)) * other, 0.0)
+            fade = jnp.exp(-rate * float(span * tokens))
+            total = jnp.where(upper, total + fade * other, other + fade * total)
+            offset = offset + jnp.where(upper, span, 0)
+            span, by = span * 2, by * 2
+    size, index = lax.axis_size(SEQ[0]), lax.axis_index(SEQ[0])
+    copies = jnp.broadcast_to(total, (size, *total.shape))
+    totals = lax.all_to_all(copies, SEQ[0], 0, 0, tiled=True)
+    fade, before = jnp.exp(-rate * float(span * tokens)), jnp.zeros_like(state)
+    for block in range(size - 1):
+        before = jnp.where(block < index, before * fade + totals[block], before)
+    return enter + jnp.exp(-rate * (offset * tokens).astype(F32)) * before
 
 
 def per_device(queries, key_proj, value_proj, decay_rate, residues, skip_gain, out_weight):
@@ -220,10 +225,9 @@
     stacked = jax.ShapeDtypeStruct((tokens * chans // LANES, LANES), F32)
     args = (key_proj, value_proj, decay_rate.T, residues.T)
     ends = jax.ShapeDtypeStruct((modes, SUBS, chans), F32)
-    rows = jax.ShapeDtypeStruct((modes * chans // LANES, LANES), F32)
-    rate, coef, ends, state, fade, mixed = whole_call(
+    rate, coef, ends, state, mixed = whole_call(
         functools.partial(state_kernel, float(tokens * seq_size)),
-        (small, small, ends, rows, rows, stacked),
+        (small, small, ends, small, stacked),
         [pltpu.VMEM(a.shape, a.dtype) for a in args] + [pltpu.SemaphoreType.DMA((len(args),))],
         ALL_VMEM,
         args,
@@ -231,7 +235,7 @@
     )
     scratch = [pltpu.VMEM(stacked.shape, F32)]
     local = whole_call(local_kernel, stacked, scratch, ALL_VMEM, (mixed, rate, coef, ends, skip_gain[None, :]))
-    enter = entering_states(state, fade)
+    enter = entering_states(state, rate, tokens)
     x_size, x_index = lax.axis_size("x"), lax.axis_index("x")
     z_size, z_index = lax.axis_size("zh"), lax.axis_index("zh").astype(jnp.int32)
     features = out_weight.shape[1] // (x_size * z_size)

time: 148 us -> 142 us (0.959)
  the two profiles are of different devices: /device:TPU:39 before, /device:TPU:6 now
where the time goes in v3:
time: 142 us; the launch traced here: 141 us
  starting transfers between devices  57.1 us (40%)
  waiting for transfers between devices  52.9 us (37%)
  Pallas kernels  22.7 us (16%)
  other arithmetic  6.56 us (5%)
  local copies, waits for them, and re-layouts  1.62 us (1%)
    ppermute x8, waiting for transfers between devices, shift(): lax.ppermute(value, axis, [(i, (i + by) % size) for i in range(size)])  42.3 us
    ppermute x8, starting transfers between devices, shift(): lax.ppermute(value, axis, [(i, (i + by) % size) for i in range(size)])  32.6 us
    pallas_call x8, Pallas kernels, whole_call(): pl.pallas_call(kernel, in_specs=in_specs or [pl.BlockSpec(memory_space=pl...  22.7 us
    ppermute x4, starting transfers between devices, entering_states(): other = lax.ppermute(total, axis, [(i, i ^ by) for i in range(size)])  20 us
    all_to_all x1, waiting for transfers between devices, entering_states(): totals = lax.all_to_all(copies, SEQ[0], 0, 0, tiled=True)  5.3 us
    ppermute x4, waiting for transfers between devices, entering_states(): other = lax.ppermute(total, axis, [(i, i ^ by) for i in range(size)])  5.25 us
    all_to_all x1, starting transfers between devices, entering_states(): totals = lax.all_to_all(copies, SEQ[0], 0, 0, tiled=True)  4.46 us
    select_n x4, other arithmetic, entering_states(): total = jnp.where(upper, total + fade * other, other + fade * total)  3.11 us
  transfers between devices with their start and end apart: 13, of which 8 were waited for; matrix products, arithmetic and copies ran while one was open for 1% of the time, Pallas kernels for 11%

profile of v3, /device:TPU:6, one launch (start us, length us, event | category | flops | bytes accessed | tf_op | source)
XLA Modules:
  0.0 141.2 jit_solution(13967407090343938251)
XLA Ops:
  0.0 3.0 %shard_map.73 = (f32[16,512]{1,0:T(8,128)}, f32[16,512]{1,0:T(8,128)}, f32[16,8,512]{2,1,0:T(8,128)}, f32[16,512]{1,0:T(8,128)}, f32[1024,128]{1,0:T(8,128)}) custom-call(bf16[256,512]{1,0:T(8,128)(2,1)} %refs_0_.1, bf16[256,512]{1,0:T(8,128)(2,1)} %refs_1_.1, f32[16,512]{1,0:T(8,128)} %bitcast.46, f32[16,512]{1,0:T(8,128)} %bitcast.47), custom_call_target="tpu_custom_call" | custom-call | flops 16777216 | bytes 2097152 | tf_op jit(solution)/shard_map/pallas_call | solution.py:31
  3.0 1.9 %collective-permute-start = (f32[16,512]{1,0:T(8,128)}, f32[16,512]{1,0:T(8,128)S(1)}, u32[]{:S(2)}, u32[]{:S(2)}) collective-permute-start(f32[16,512]{1,0:T(8,128)} %get-tuple-element.23), channel_id=1, source_target_pairs={{0,8},{8,0},{1,9},{9,1},{2,10},{10,2},{3,11},{11,3},{4,12},{12,4},... | collective-permute-start | bytes 98312 | tf_op jit(solution)/shard_map/ppermute | solution.py:202
  4.9 1.4 collective-permute-done
  6.3 0.8 add_select_fusion.3
  7.1 3.8 %collective-permute-start.1 = (f32[16,512]{1,0:T(8,128)S(1)}, f32[16,512]{1,0:T(8,128)S(1)}, u32[]{:S(2)}, u32[]{:S(2)}) collective-permute-start(f32[16,512]{1,0:T(8,128)S(1)} %add_select_fusion.3), channel_id=1, source_target_pairs={{0,16},{16,0},{32,48},{48,32},{64,80},{80,64},{96,112},{112,96},{1... | collective-permute-start | bytes 98312 | tf_op jit(solution)/shard_map/ppermute | solution.py:202
  10.9 2.0 %collective-permute-done.1 = f32[16,512]{1,0:T(8,128)S(1)} collective-permute-done((f32[16,512]{1,0:T(8,128)S(1)}, f32[16,512]{1,0:T(8,128)S(1)}, u32[]{:S(2)}, u32[]{:S(2)}) %collective-permute-start.1) | collective-permute-done | bytes 32800 | tf_op jit(solution)/shard_map/ppermute | solution.py:202
  13.7 5.2 %collective-permute-start.2 = (f32[16,512]{1,0:T(8,128)S(1)}, f32[16,512]{1,0:T(8,128)S(1)}, u32[]{:S(2)}, u32[]{:S(2)}) collective-permute-start(f32[16,512]{1,0:T(8,128)S(1)} %add_select_fusion.2), channel_id=1, source_target_pairs={{0,32},{16,48},{32,0},{48,16},{64,96},{80,112},{96,64},{112,80},{1... | collective-permute-start | bytes 98312 | tf_op jit(solution)/shard_map/ppermute | solution.py:202
  18.9 1.9 %collective-permute-done.2 = f32[16,512]{1,0:T(8,128)S(1)} collective-permute-done((f32[16,512]{1,0:T(8,128)S(1)}, f32[16,512]{1,0:T(8,128)S(1)}, u32[]{:S(2)}, u32[]{:S(2)}) %collective-permute-start.2) | collective-permute-done | bytes 32800 | tf_op jit(solution)/shard_map/ppermute | solution.py:202
  21.5 9.1 %collective-permute-start.3 = (f32[16,512]{1,0:T(8,128)S(1)}, f32[16,512]{1,0:T(8,128)S(1)}, u32[]{:S(2)}, u32[]{:S(2)}) collective-permute-start(f32[16,512]{1,0:T(8,128)S(1)} %add_select_fusion.1), channel_id=1, source_target_pairs={{0,64},{16,80},{32,96},{48,112},{64,0},{80,16},{96,32},{112,48},{1... | collective-permute-start | bytes 98312 | tf_op jit(solution)/shard_map/ppermute | solution.py:202
  30.7 4.0 %shard_map.74.local_ref = f32[1024,128]{1,0:T(8,128)} custom-call(f32[1024,128]{1,0:T(8,128)} %get-tuple-element.19.x_ref, f32[16,512]{1,0:T(8,128)} %get-tuple-element.20.rate_ref, f32[16,512]{1,0:T(8,128)} %get-tuple-element.21.coef_ref, f32[16,8,512]{2,1,0:T(8,128)} %get-tuple-element.22.ends_ref, f32[1,512]{1,0:T(1,128)} %bitcast.48), custom_call_target="tpu_custom_call" | custom-call | flops 16777216 | bytes 2097152 | tf_op jit(solution)/shard_map/pallas_call | solution.py:31
  36.2 4.5 %all-to-all-start = ((f32[4,16,512]{2,1,0:T(8,128)}), f32[4,16,512]{2,1,0:T(8,128)S(1)}, u32[]{:S(2)}, u32[]{:S(2)}) async-start(f32[4,16,512]{2,1,0:T(8,128)} %broadcast_in_dim.17), calls=%async_computation | async-start | bytes 262144 | tf_op jit(solution)/shard_map/all_to_all | solution.py:211
  41.3 5.3 %all-to-all-done = f32[4,16,512]{2,1,0:T(8,128)S(1)} async-done(((f32[4,16,512]{2,1,0:T(8,128)}), f32[4,16,512]{2,1,0:T(8,128)S(1)}, u32[]{:S(2)}, u32[]{:S(2)}) %all-to-all-start) | async-done | bytes 131104 | tf_op jit(solution)/shard_map/all_to_all | solution.py:211
  46.6 1.4 %fusion.3.enter_ref = f32[16,512]{1,0:T(8,128)} fusion(f32[4,16,512]{2,1,0:T(8,128)S(1)} %all-to-all-done, f32[16,512]{1,0:T(8,128)S(1)} %collective-permute-done.3, f32[16,512]{1,0:T(8,128)S(1)} %collective-permute-done.2, f32[16,512]{1,0:T(8,128)S(1)} %collective-permute-done.1, f32[16,512]{1,0:T(8,128)S(1)} %collective-permute-done, ...), kind=kLoop, calls=%fused_computation.7 | loop fusion | flops 237568 | bytes 294935 | tf_op jit(solution)/shard_map/add | solution.py:215
  48.0 4.1 %shard_map.75 = (bf16[256,512]{1,0:T(8,128)(2,1)}, f32[2,256,256]{2,1,0:T(8,128)}, f32[2,256,256]{2,1,0:T(8,128)}) custom-call(s32[4]{0:T(128)} %and_select_fusion.4.cols_ref, bf16[256,512]{1,0:T(8,128)(2,1)} %q_ref.1, f32[1024,128]{1,0:T(8,128)} %shard_map.74.local_ref, f32[16,512]{1,0:T(8,128)} %get-tuple-element.20.rate_ref, ...), custom_call_target="tpu_custom_call" | custom-call | flops 16777216 | bytes 2097152 | tf_op jit(solution)/shard_map/pallas_call | solution.py:31
  52.1 3.3 %collective-permute-start.4 = (f32[2,256,256]{2,1,0:T(8,128)}, f32[2,256,256]{2,1,0:T(8,128)S(1)}, u32[]{:S(2)}, u32[]{:S(2)}) collective-permute-start(f32[2,256,256]{2,1,0:T(8,128)} %get-tuple-element.25), channel_id=1, source_target_pairs={{0,2},{2,4},{4,6},{6,0},{1,3},{3,5},{5,7},{7,1},{8,10},{10,12},{12... | collective-permute-start | bytes 1572872 | tf_op jit(solution)/shard_map/ppermute | solution.py:192
  55.5 0.9 copy-done
  56.4 3.2 %shard_map.78 = (f32[2,256,256]{2,1,0:T(8,128)}, f32[2,256,256]{2,1,0:T(8,128)S(1)}) custom-call(s32[4]{0:T(128)S(1)} %and_select_fusion.cols_ref, bf16[256,512]{1,0:T(8,128)(2,1)S(1)} %copy-done, bf16[512,4096]{1,0:T(8,128)(2,1)} %weight_ref.11), custom_call_target="tpu_custom_call" | custom-call | flops 16777216 | bytes 2097152 | tf_op jit(solution)/shard_map/pallas_call | solution.py:31
  59.6 2.6 %collective-permute-start.8 = (f32[2,256,256]{2,1,0:T(8,128)}, f32[2,256,256]{2,1,0:T(8,128)S(1)}, u32[]{:S(2)}, u32[]{:S(2)}) collective-permute-start(f32[2,256,256]{2,1,0:T(8,128)} %get-tuple-element.29), channel_id=1, source_target_pairs={{0,6},{2,0},{4,2},{6,4},{1,7},{3,1},{5,3},{7,5},{8,14},{10,8},{12,... | collective-permute-start | bytes 1572872 | tf_op jit(solution)/shard_map/ppermute | solution.py:192
  62.3 2.7 %collective-permute-start.6 = (f32[2,256,256]{2,1,0:T(8,128)}, f32[2,256,256]{2,1,0:T(8,128)S(1)}, u32[]{:S(2)}, u32[]{:S(2)}) collective-permute-start(f32[2,256,256]{2,1,0:T(8,128)} %get-tuple-element.26), channel_id=1, source_target_pairs={{0,6},{2,0},{4,2},{6,4},{1,7},{3,1},{5,3},{7,5},{8,14},{10,8},{12,... | collective-permute-start | bytes 1572872 | tf_op jit(solution)/shard_map/ppermute | solution.py:192
  65.1 2.1 %shard_map.76 = f32[2,256,256]{2,1,0:T(8,128)S(1)} custom-call(s32[2]{0:T(128)S(1)} %and_select_fusion.3.cols_ref, bf16[256,512]{1,0:T(8,128)(2,1)S(1)} %copy-done, bf16[512,4096]{1,0:T(8,128)(2,1)} %weight_ref.11, f32[2,256,256]{2,1,0:T(8,128)S(1)} %collective-permute-done.4.refs_0_), custom_call_target="tpu_custom_call" | custom-call | flops 16777216 | bytes 2097152 | tf_op jit(solution)/shard_map/pallas_call | solution.py:31
  67.2 4.3 %collective-permute-start.5 = (f32[2,256,256]{2,1,0:T(8,128)S(1)}, f32[2,256,256]{2,1,0:T(8,128)S(1)}, u32[]{:S(2)}, u32[]{:S(2)}) collective-permute-start(f32[2,256,256]{2,1,0:T(8,128)S(1)} %shard_map.76), channel_id=1, source_target_pairs={{0,2},{2,4},{4,6},{6,0},{1,3},{3,5},{5,7},{7,1},{8,10},{10,12},{12... | collective-permute-start | bytes 1572872 | tf_op jit(solution)/shard_map/ppermute | solution.py:192
  71.6 3.2 %collective-permute-start.10 = (f32[2,256,256]{2,1,0:T(8,128)}, f32[2,256,256]{2,1,0:T(8,128)S(1)}, u32[]{:S(2)}, u32[]{:S(2)}) collective-permute-start(f32[2,256,256]{2,1,0:T(8,128)} %copy-done.2), channel_id=1, source_target_pairs={{0,2},{2,4},{4,6},{6,0},{1,3},{3,5},{5,7},{7,1},{8,10},{10,12},{12... | collective-permute-start | bytes 1572872 | tf_op jit(solution)/shard_map/ppermute | solution.py:192
  74.8 3.0 %collective-permute-done.8.refs_0_ = f32[2,256,256]{2,1,0:T(8,128)S(1)} collective-permute-done((f32[2,256,256]{2,1,0:T(8,128)}, f32[2,256,256]{2,1,0:T(8,128)S(1)}, u32[]{:S(2)}, u32[]{:S(2)}) %collective-permute-start.8) | collective-permute-done | bytes 524320 | tf_op jit(solution)/shard_map/ppermute | solution.py:192
  77.8 2.1 %shard_map.79 = f32[2,256,256]{2,1,0:T(8,128)S(1)} custom-call(s32[2]{0:T(128)S(1)} %and_select_fusion.1.cols_ref, bf16[256,512]{1,0:T(8,128)(2,1)S(1)} %copy-done.1, bf16[512,4096]{1,0:T(8,128)(2,1)} %weight_ref.11, f32[2,256,256]{2,1,0:T(8,128)S(1)} %collective-permute-done.8.refs_0_), custom_call_target="tpu_custom_call" | custom-call | flops 16777216 | bytes 2097152 | tf_op jit(solution)/shard_map/pallas_call | solution.py:31
  79.9 1.9 %collective-permute-start.9 = (f32[2,256,256]{2,1,0:T(8,128)S(1)}, f32[2,256,256]{2,1,0:T(8,128)S(1)}, u32[]{:S(2)}, u32[]{:S(2)}) collective-permute-start(f32[2,256,256]{2,1,0:T(8,128)S(1)} %shard_map.79), channel_id=1, source_target_pairs={{0,6},{2,0},{4,2},{6,4},{1,7},{3,1},{5,3},{7,5},{8,14},{10,8},{12,... | collective-permute-start | bytes 1572872 | tf_op jit(solution)/shard_map/ppermute | solution.py:192
  82.0 7.0 %collective-permute-done.6.right_ref = f32[2,256,256]{2,1,0:T(8,128)S(1)} collective-permute-done((f32[2,256,256]{2,1,0:T(8,128)}, f32[2,256,256]{2,1,0:T(8,128)S(1)}, u32[]{:S(2)}, u32[]{:S(2)}) %collective-permute-start.6) | collective-permute-done | bytes 524320 | tf_op jit(solution)/shard_map/ppermute | solution.py:192
  89.1 2.2 %shard_map.77 = (f32[256,256]{1,0:T(8,128)S(1)}, f32[256,256]{1,0:T(8,128)S(1)}) custom-call(s32[3]{0:T(128)S(1)} %pad_add_fusion.1.cols_ref, bf16[256,512]{1,0:T(8,128)(2,1)S(1)} %copy-done.1, bf16[512,4096]{1,0:T(8,128)(2,1)} %weight_ref.11, f32[2,256,256]{2,1,0:T(8,128)S(1)} %collective-permute-done.5.left_ref, ...), custom_call_target="tpu_custom_call" | custom-call | flops 16777216 | bytes 2097152 | tf_op jit(solution)/shard_map/pallas_call | solution.py:31
  91.2 10.6 %collective-permute-start.7 = (f32[256,256]{1,0:T(8,128)S(1)}, f32[256,256]{1,0:T(8,128)S(1)}, u32[]{:S(2)}, u32[]{:S(2)}) collective-permute-start(f32[256,256]{1,0:T(8,128)S(1)} %get-tuple-element.28), channel_id=1, source_target_pairs={{0,1},{1,0},{2,3},{3,2},{4,5},{5,4},{6,7},{7,6},{8,9},{9,8},{10,11... | collective-permute-start | bytes 786440 | tf_op jit(solution)/shard_map/ppermute | solution.py:192
  102.0 2.2 %shard_map.80 = (f32[256,256]{1,0:T(8,128)S(1)}, f32[256,256]{1,0:T(8,128)S(1)}) custom-call(s32[3]{0:T(128)S(1)} %pad_add_fusion.5.cols_ref, bf16[256,512]{1,0:T(8,128)(2,1)S(1)} %copy-done.1, bf16[512,4096]{1,0:T(8,128)(2,1)} %weight_ref.11, f32[2,256,256]{2,1,0:T(8,128)S(1)} %collective-permute-done.9.left_ref, ...), custom_call_target="tpu_custom_call" | custom-call | flops 16777216 | bytes 2097152 | tf_op jit(solution)/shard_map/pallas_call | solution.py:31
  104.2 4.0 %collective-permute-start.11 = (f32[256,256]{1,0:T(8,128)S(1)}, f32[256,256]{1,0:T(8,128)S(1)}, u32[]{:S(2)}, u32[]{:S(2)}) collective-permute-start(f32[256,256]{1,0:T(8,128)S(1)} %get-tuple-element.32), channel_id=1, source_target_pairs={{0,1},{1,0},{2,3},{3,2},{4,5},{5,4},{6,7},{7,6},{8,9},{9,8},{10,11... | collective-permute-start | bytes 786440 | tf_op jit(solution)/shard_map/ppermute | solution.py:192
  108.2 25.6 %collective-permute-done.7 = f32[256,256]{1,0:T(8,128)S(1)} collective-permute-done((f32[256,256]{1,0:T(8,128)S(1)}, f32[256,256]{1,0:T(8,128)S(1)}, u32[]{:S(2)}, u32[]{:S(2)}) %collective-permute-start.7) | collective-permute-done | bytes 262176 | tf_op jit(solution)/shard_map/ppermute | solution.py:192
  133.8 6.7 %collective-permute-done.11 = f32[256,256]{1,0:T(8,128)S(1)} collective-permute-done((f32[256,256]{1,0:T(8,128)S(1)}, f32[256,256]{1,0:T(8,128)S(1)}, u32[]{:S(2)}, u32[]{:S(2)}) %collective-permute-start.11) | collective-permute-done | bytes 262176 | tf_op jit(solution)/shard_map/ppermute | solution.py:192
  (25 shorter events, 5.0 us)
Async XLA Ops:
  3.0 3.3 %collective-permute-start = (f32[16,512]{1,0:T(8,128)}, f32[16,512]{1,0:T(8,128)S(1)}, u32[]{:S(2)}, u32[]{:S(2)}) collective-permute-start(f32[16,512]{1,0:T(8,128)} %get-tuple-element.23), channel_id=1, source_target_pairs={{0,8},{8,0},{1,9},{9,1},{2,10},{10,2},{3,11},{11,3},{4,12},{12,4},... | collective-permute-start | bytes 98312 | tf_op jit(solution)/shard_map/ppermute | solution.py:202
  7.1 5.8 %collective-permute-start.1 = (f32[16,512]{1,0:T(8,128)S(1)}, f32[16,512]{1,0:T(8,128)S(1)}, u32[]{:S(2)}, u32[]{:S(2)}) collective-permute-start(f32[16,512]{1,0:T(8,128)S(1)} %add_select_fusion.3), channel_id=1, source_target_pairs={{0,16},{16,0},{32,48},{48,32},{64,80},{80,64},{96,112},{112,96},{1... | collective-permute-start | bytes 98312 | tf_op jit(solution)/shard_map/ppermute | solution.py:202
  13.7 7.1 %collective-permute-start.2 = (f32[16,512]{1,0:T(8,128)S(1)}, f32[16,512]{1,0:T(8,128)S(1)}, u32[]{:S(2)}, u32[]{:S(2)}) collective-permute-start(f32[16,512]{1,0:T(8,128)S(1)} %add_select_fusion.2), channel_id=1, source_target_pairs={{0,32},{16,48},{32,0},{48,16},{64,96},{80,112},{96,64},{112,80},{1... | collective-permute-start | bytes 98312 | tf_op jit(solution)/shard_map/ppermute | solution.py:202
  21.5 13.2 %collective-permute-start.3 = (f32[16,512]{1,0:T(8,128)S(1)}, f32[16,512]{1,0:T(8,128)S(1)}, u32[]{:S(2)}, u32[]{:S(2)}) collective-permute-start(f32[16,512]{1,0:T(8,128)S(1)} %add_select_fusion.1), channel_id=1, source_target_pairs={{0,64},{16,80},{32,96},{48,112},{64,0},{80,16},{96,32},{112,48},{1... | collective-permute-start | bytes 98312 | tf_op jit(solution)/shard_map/ppermute | solution.py:202
  36.2 10.4 %all-to-all-start = ((f32[4,16,512]{2,1,0:T(8,128)}), f32[4,16,512]{2,1,0:T(8,128)S(1)}, u32[]{:S(2)}, u32[]{:S(2)}) async-start(f32[4,16,512]{2,1,0:T(8,128)} %broadcast_in_dim.17), calls=%async_computation | async-start | bytes 262144 | tf_op jit(solution)/shard_map/all_to_all | solution.py:211
  52.1 13.0 %collective-permute-start.4 = (f32[2,256,256]{2,1,0:T(8,128)}, f32[2,256,256]{2,1,0:T(8,128)S(1)}, u32[]{:S(2)}, u32[]{:S(2)}) collective-permute-start(f32[2,256,256]{2,1,0:T(8,128)} %get-tuple-element.25), channel_id=1, source_target_pairs={{0,2},{2,4},{4,6},{6,0},{1,3},{3,5},{5,7},{7,1},{8,10},{10,12},{12... | collective-permute-start | bytes 1572872 | tf_op jit(solution)/shard_map/ppermute | solution.py:192
  55.5 1.0 copy-start
  56.4 21.4 %copy-start.1 = (bf16[256,512]{1,0:T(8,128)(2,1)S(1)}, bf16[256,512]{1,0:T(8,128)(2,1)}, u32[]{:S(2)}) copy-start(bf16[256,512]{1,0:T(8,128)(2,1)} %get-tuple-element.24.gated_ref) | copy-start | bytes 786436
  59.6 7.5 %copy-start.2 = (f32[2,256,256]{2,1,0:T(8,128)}, f32[2,256,256]{2,1,0:T(8,128)S(1)}, u32[]{:S(2)}) copy-start(f32[2,256,256]{2,1,0:T(8,128)S(1)} %get-tuple-element.30) | copy-start | bytes 1572868
  59.6 18.2 %collective-permute-start.8 = (f32[2,256,256]{2,1,0:T(8,128)}, f32[2,256,256]{2,1,0:T(8,128)S(1)}, u32[]{:S(2)}, u32[]{:S(2)}) collective-permute-start(f32[2,256,256]{2,1,0:T(8,128)} %get-tuple-element.29), channel_id=1, source_target_pairs={{0,6},{2,0},{4,2},{6,4},{1,7},{3,1},{5,3},{7,5},{8,14},{10,8},{12,... | collective-permute-start | bytes 1572872 | tf_op jit(solution)/shard_map/ppermute | solution.py:192
  62.3 26.7 %collective-permute-start.6 = (f32[2,256,256]{2,1,0:T(8,128)}, f32[2,256,256]{2,1,0:T(8,128)S(1)}, u32[]{:S(2)}, u32[]{:S(2)}) collective-permute-start(f32[2,256,256]{2,1,0:T(8,128)} %get-tuple-element.26), channel_id=1, source_target_pairs={{0,6},{2,0},{4,2},{6,4},{1,7},{3,1},{5,3},{7,5},{8,14},{10,8},{12,... | collective-permute-start | bytes 1572872 | tf_op jit(solution)/shard_map/ppermute | solution.py:192
  67.2 21.9 %collective-permute-start.5 = (f32[2,256,256]{2,1,0:T(8,128)S(1)}, f32[2,256,256]{2,1,0:T(8,128)S(1)}, u32[]{:S(2)}, u32[]{:S(2)}) collective-permute-start(f32[2,256,256]{2,1,0:T(8,128)S(1)} %shard_map.76), channel_id=1, source_target_pairs={{0,2},{2,4},{4,6},{6,0},{1,3},{3,5},{5,7},{7,1},{8,10},{10,12},{12... | collective-permute-start | bytes 1572872 | tf_op jit(solution)/shard_map/ppermute | solution.py:192
  71.6 30.4 %collective-permute-start.10 = (f32[2,256,256]{2,1,0:T(8,128)}, f32[2,256,256]{2,1,0:T(8,128)S(1)}, u32[]{:S(2)}, u32[]{:S(2)}) collective-permute-start(f32[2,256,256]{2,1,0:T(8,128)} %copy-done.2), channel_id=1, source_target_pairs={{0,2},{2,4},{4,6},{6,0},{1,3},{3,5},{5,7},{7,1},{8,10},{10,12},{12... | collective-permute-start | bytes 1572872 | tf_op jit(solution)/shard_map/ppermute | solution.py:192
  79.9 22.1 %collective-permute-start.9 = (f32[2,256,256]{2,1,0:T(8,128)S(1)}, f32[2,256,256]{2,1,0:T(8,128)S(1)}, u32[]{:S(2)}, u32[]{:S(2)}) collective-permute-start(f32[2,256,256]{2,1,0:T(8,128)S(1)} %shard_map.79), channel_id=1, source_target_pairs={{0,6},{2,0},{4,2},{6,4},{1,7},{3,1},{5,3},{7,5},{8,14},{10,8},{12,... | collective-permute-start | bytes 1572872 | tf_op jit(solution)/shard_map/ppermute | solution.py:192
  91.2 42.5 %collective-permute-start.7 = (f32[256,256]{1,0:T(8,128)S(1)}, f32[256,256]{1,0:T(8,128)S(1)}, u32[]{:S(2)}, u32[]{:S(2)}) collective-permute-start(f32[256,256]{1,0:T(8,128)S(1)} %get-tuple-element.28), channel_id=1, source_target_pairs={{0,1},{1,0},{2,3},{3,2},{4,5},{5,4},{6,7},{7,6},{8,9},{9,8},{10,11... | collective-permute-start | bytes 786440 | tf_op jit(solution)/shard_map/ppermute | solution.py:192
  104.2 36.3 %collective-permute-start.11 = (f32[256,256]{1,0:T(8,128)S(1)}, f32[256,256]{1,0:T(8,128)S(1)}, u32[]{:S(2)}, u32[]{:S(2)}) collective-permute-start(f32[256,256]{1,0:T(8,128)S(1)} %get-tuple-element.32), channel_id=1, source_target_pairs={{0,1},{1,0},{2,3},{3,2},{4,5},{5,4},{6,7},{7,6},{8,9},{9,8},{10,11... | collective-permute-start | bytes 786440 | tf_op jit(solution)/shard_map/ppermute | solution.py:192

commit v4 on v3

--- a/solution.py
+++ b/solution.py
@@ -195,24 +195,21 @@
 def entering_states(state, rate, tokens):
     enter, total = jnp.zeros_like(state), state
     offset, span = jnp.int32(0), 1
-    for axis in reversed(SEQ[1:]):
+    for axis in reversed(SEQ):
         size, index = lax.axis_size(axis), lax.axis_index(axis)
-        by = 1
-        while by < size:
-            other = lax.ppermute(total, axis, [(i, i ^ by) for i in range(size)])
-            upper = (index & by) != 0
-            enter = enter + jnp.where(upper, jnp.exp(-rate * (offset * tokens).astype(F32)) * other, 0.0)
-            fade = jnp.exp(-rate * float(span * tokens))
-            total = jnp.where(upper, total + fade * other, other + fade * total)
-            offset = offset + jnp.where(upper, span, 0)
-            span, by = span * 2, by * 2
-    size, index = lax.axis_size(SEQ[0]), lax.axis_index(SEQ[0])
-    copies = jnp.broadcast_to(total, (size, *total.shape))
-    totals = lax.all_to_all(copies, SEQ[0], 0, 0, tiled=True)
-    fade, before = jnp.exp(-rate * float(span * tokens)), jnp.zeros_like(state)
-    for block in range(size - 1):
-        before = jnp.where(block < index, before * fade + totals[block], before)
-    return enter + jnp.exp(-rate * (offset * tokens).astype(F32)) * before
+        if size == 2:
+            other = lax.ppermute(total, axis, [(0, 1), (1, 0)])
+            totals = [jnp.where(index == 0, total, other), jnp.where(index == 0, other, total)]
+        else:
+            copies = jnp.broadcast_to(total, (size, *total.shape))
+            totals = lax.all_to_all(copies, axis, 0, 0, tiled=True)
+        fade, before, total = jnp.exp(-rate * float(span * tokens)), jnp.zeros_like(state), jnp.zeros_like(state)
+        for block in range(size):
+            before = jnp.where(block == index, total, before)
+            total = total * fade + totals[block]
+        enter = enter + jnp.exp(-rate * (offset * tokens).astype(F32)) * before
+        offset, span = offset + index * span, span * size
+    return enter
 
 
 def per_device(queries, key_proj, value_proj, decay_rate, residues, skip_gain, out_weight):

time: 142 us -> 146 us (1.028)
  waiting for transfers between devices: 52.9 us -> 63.6 us
  starting transfers between devices: 57.1 us -> 51 us
  other arithmetic: 6.56 us -> 4.97 us
    ppermute x4 -> x1, starting transfers between devices: 20 us -> 1.92 us  [entering_states(): other = lax.ppermute(total, axis, [(0, 1), (1, 0)])]
    all_to_all x1 -> x2, waiting for transfers between devices: 5.3 us -> 18.4 us  [entering_states(): totals = lax.all_to_all(copies, axis, 0, 0, tiled=True)]
    all_to_all x1 -> x2, starting transfers between devices: 4.46 us -> 17 us  [entering_states(): totals = lax.all_to_all(copies, axis, 0, 0, tiled=True)]
    ppermute x4 -> x1, waiting for transfers between devices: 5.25 us -> 1.38 us  [entering_states(): other = lax.ppermute(total, axis, [(0, 1), (1, 0)])]
    select_n x4 -> x0, other arithmetic: 3.11 us -> none  [entering_states(): total = jnp.where(upper, total + fade * other, other + fade * total)]
    add x1 -> x3, other arithmetic: 1.41 us -> 3.05 us  [the longest x2 1.58 us: entering_states(): total = total * fade + totals[block]]
    ppermute x8, waiting for transfers between devices: 42.3 us -> 43.8 us  [shift(): lax.ppermute(value, axis, [(i, (i + by) % size) for i in range(size)])]
  transfers between devices with their start and end apart: 13 -> 11, of which waited for: 8 -> 7; matrix products, arithmetic and copies ran while one was open for 1% -> 1% of each run, Pallas kernels for 11% -> 11%
where the time goes in v4:
time: 146 us; the launch traced here: 145 us
  waiting for transfers between devices  63.6 us (44%)
  starting transfers between devices  51 us (35%)
  Pallas kernels  22.7 us (16%)
  other arithmetic  4.97 us (3%)
  local copies, waits for them, and re-layouts  2.35 us (2%)
    ppermute x8, waiting for transfers between devices, shift(): lax.ppermute(value, axis, [(i, (i + by) % size) for i in range(size)])  43.8 us
    ppermute x8, starting transfers between devices, shift(): lax.ppermute(value, axis, [(i, (i + by) % size) for i in range(size)])  32.1 us
    pallas_call x8, Pallas kernels, whole_call(): pl.pallas_call(kernel, in_specs=in_specs or [pl.BlockSpec(memory_space=pl...  22.7 us
    all_to_all x2, waiting for transfers between devices, entering_states(): totals = lax.all_to_all(copies, axis, 0, 0, tiled=True)  18.4 us
    all_to_all x2, starting transfers between devices, entering_states(): totals = lax.all_to_all(copies, axis, 0, 0, tiled=True)  17 us
  transfers between devices with their start and end apart: 11, of which 7 were waited for; matrix products, arithmetic and copies ran while one was open for 1% of the time, Pallas kernels for 11%

profile of v4, /device:TPU:6, one launch (start us, length us, event | category | flops | bytes accessed | tf_op | source)
XLA Modules:
  0.0 144.9 jit_solution(1569058103376790176)
XLA Ops:
  0.0 3.0 %shard_map.73 = (f32[16,512]{1,0:T(8,128)}, f32[16,512]{1,0:T(8,128)}, f32[16,8,512]{2,1,0:T(8,128)}, f32[16,512]{1,0:T(8,128)}, f32[1024,128]{1,0:T(8,128)}) custom-call(bf16[256,512]{1,0:T(8,128)(2,1)} %refs_0_.1, bf16[256,512]{1,0:T(8,128)(2,1)} %refs_1_.1, f32[16,512]{1,0:T(8,128)} %bitcast.122, f32[16,512]{1,0:T(8,128)} %bitcast.123), custom_call_target="tpu_custom_call" | custom-call | flops 16777216 | bytes 2097152 | tf_op jit(solution)/shard_map/pallas_call | solution.py:31
  3.0 1.9 %collective-permute-start = (f32[16,512]{1,0:T(8,128)}, f32[16,512]{1,0:T(8,128)S(1)}, u32[]{:S(2)}, u32[]{:S(2)}) collective-permute-start(f32[16,512]{1,0:T(8,128)} %get-tuple-element.23), channel_id=1, source_target_pairs={{0,8},{8,0},{1,9},{9,1},{2,10},{10,2},{3,11},{11,3},{4,12},{12,4},... | collective-permute-start | bytes 98312 | tf_op jit(solution)/shard_map/ppermute | solution.py:201
  4.9 1.4 collective-permute-done
  6.3 0.8 select_add_fusion
  7.1 0.7 broadcast_in_dim.15
  7.8 12.5 %all-to-all-start = ((f32[8,16,512]{2,1,0:T(8,128)}), f32[8,16,512]{2,1,0:T(8,128)S(1)}, u32[]{:S(2)}, u32[]{:S(2)}) async-start(f32[8,16,512]{2,1,0:T(8,128)} %broadcast_in_dim.15), calls=%async_computation | async-start | bytes 524288 | tf_op jit(solution)/shard_map/all_to_all | solution.py:205
  20.3 4.0 %shard_map.74.local_ref = f32[1024,128]{1,0:T(8,128)} custom-call(f32[1024,128]{1,0:T(8,128)} %get-tuple-element.19.x_ref, f32[16,512]{1,0:T(8,128)} %get-tuple-element.20.rate_ref, f32[16,512]{1,0:T(8,128)} %get-tuple-element.21.coef_ref, f32[16,8,512]{2,1,0:T(8,128)} %get-tuple-element.22.ends_ref, f32[1,512]{1,0:T(1,128)} %bitcast.124), custom_call_target="tpu_custom_call" | custom-call | flops 16777216 | bytes 2097152 | tf_op jit(solution)/shard_map/pallas_call | solution.py:31
  24.3 13.0 %all-to-all-done = f32[8,16,512]{2,1,0:T(8,128)S(1)} async-done(((f32[8,16,512]{2,1,0:T(8,128)}), f32[8,16,512]{2,1,0:T(8,128)S(1)}, u32[]{:S(2)}, u32[]{:S(2)}) %all-to-all-start) | async-done | bytes 262176 | tf_op jit(solution)/shard_map/all_to_all | solution.py:205
  37.3 0.8 fusion.6
  38.8 4.5 %all-to-all-start.1 = ((f32[4,16,512]{2,1,0:T(8,128)}), f32[4,16,512]{2,1,0:T(8,128)S(1)}, u32[]{:S(2)}, u32[]{:S(2)}) async-start(f32[4,16,512]{2,1,0:T(8,128)} %broadcast_in_dim.16), calls=%async_computation.1 | async-start | bytes 262144 | tf_op jit(solution)/shard_map/all_to_all | solution.py:205
  43.8 5.4 %all-to-all-done.1 = f32[4,16,512]{2,1,0:T(8,128)S(1)} async-done(((f32[4,16,512]{2,1,0:T(8,128)}), f32[4,16,512]{2,1,0:T(8,128)S(1)}, u32[]{:S(2)}, u32[]{:S(2)}) %all-to-all-start.1) | async-done | bytes 131104 | tf_op jit(solution)/shard_map/all_to_all | solution.py:205
  49.2 1.5 %fusion.3.enter_ref = f32[16,512]{1,0:T(8,128)} fusion(f32[4,16,512]{2,1,0:T(8,128)S(1)} %all-to-all-done.1, f32[16,512]{1,0:T(8,128)} %get-tuple-element.23, f32[16,512]{1,0:T(8,128)S(1)} %collective-permute-done, f32[16,512]{1,0:T(8,128)} %get-tuple-element.20.rate_ref, f32[8,16,512]{2,1,0:T(8,128)S(1)} %all-to-all-done, f32[]{:T(128)S(6)} %convert_element_type.8, ...), kind=kLoop, calls=%fused_computation.7 | loop fusion | flops 376832 | bytes 458772 | tf_op jit(solution)/shard_map/add | solution.py:210
  50.7 4.1 %shard_map.75 = (bf16[256,512]{1,0:T(8,128)(2,1)}, f32[2,256,256]{2,1,0:T(8,128)}, f32[2,256,256]{2,1,0:T(8,128)}) custom-call(s32[4]{0:T(128)} %and_select_fusion.4.cols_ref, bf16[256,512]{1,0:T(8,128)(2,1)} %q_ref.1, f32[1024,128]{1,0:T(8,128)} %shard_map.74.local_ref, f32[16,512]{1,0:T(8,128)} %get-tuple-element.20.rate_ref, ...), custom_call_target="tpu_custom_call" | custom-call | flops 16777216 | bytes 2097152 | tf_op jit(solution)/shard_map/pallas_call | solution.py:31
  54.7 2.4 %collective-permute-start.1 = (f32[2,256,256]{2,1,0:T(8,128)}, f32[2,256,256]{2,1,0:T(8,128)S(1)}, u32[]{:S(2)}, u32[]{:S(2)}) collective-permute-start(f32[2,256,256]{2,1,0:T(8,128)} %get-tuple-element.25), channel_id=1, source_target_pairs={{0,2},{2,4},{4,6},{6,0},{1,3},{3,5},{5,7},{7,1},{8,10},{10,12},{12... | collective-permute-start | bytes 1572872 | tf_op jit(solution)/shard_map/ppermute | solution.py:192
  57.2 0.9 copy-done
  58.2 3.2 %shard_map.78 = (f32[2,256,256]{2,1,0:T(8,128)}, f32[2,256,256]{2,1,0:T(8,128)S(1)}) custom-call(s32[4]{0:T(128)S(1)} %and_select_fusion.cols_ref, bf16[256,512]{1,0:T(8,128)(2,1)S(1)} %copy-done, bf16[512,4096]{1,0:T(8,128)(2,1)} %weight_ref.11), custom_call_target="tpu_custom_call" | custom-call | flops 16777216 | bytes 2097152 | tf_op jit(solution)/shard_map/pallas_call | solution.py:31
  61.4 3.5 %collective-permute-start.5 = (f32[2,256,256]{2,1,0:T(8,128)}, f32[2,256,256]{2,1,0:T(8,128)S(1)}, u32[]{:S(2)}, u32[]{:S(2)}) collective-permute-start(f32[2,256,256]{2,1,0:T(8,128)} %get-tuple-element.29), channel_id=1, source_target_pairs={{0,6},{2,0},{4,2},{6,4},{1,7},{3,1},{5,3},{7,5},{8,14},{10,8},{12,... | collective-permute-start | bytes 1572872 | tf_op jit(solution)/shard_map/ppermute | solution.py:192
  65.0 2.7 %collective-permute-start.3 = (f32[2,256,256]{2,1,0:T(8,128)}, f32[2,256,256]{2,1,0:T(8,128)S(1)}, u32[]{:S(2)}, u32[]{:S(2)}) collective-permute-start(f32[2,256,256]{2,1,0:T(8,128)} %get-tuple-element.26), channel_id=1, source_target_pairs={{0,6},{2,0},{4,2},{6,4},{1,7},{3,1},{5,3},{7,5},{8,14},{10,8},{12,... | collective-permute-start | bytes 1572872 | tf_op jit(solution)/shard_map/ppermute | solution.py:192
  67.7 2.1 %shard_map.76 = f32[2,256,256]{2,1,0:T(8,128)S(1)} custom-call(s32[2]{0:T(128)S(1)} %and_select_fusion.3.cols_ref, bf16[256,512]{1,0:T(8,128)(2,1)S(1)} %copy-done, bf16[512,4096]{1,0:T(8,128)(2,1)} %weight_ref.11, f32[2,256,256]{2,1,0:T(8,128)S(1)} %collective-permute-done.1.refs_0_), custom_call_target="tpu_custom_call" | custom-call | flops 16777216 | bytes 2097152 | tf_op jit(solution)/shard_map/pallas_call | solution.py:31
  69.8 4.3 %collective-permute-start.2 = (f32[2,256,256]{2,1,0:T(8,128)S(1)}, f32[2,256,256]{2,1,0:T(8,128)S(1)}, u32[]{:S(2)}, u32[]{:S(2)}) collective-permute-start(f32[2,256,256]{2,1,0:T(8,128)S(1)} %shard_map.76), channel_id=1, source_target_pairs={{0,2},{2,4},{4,6},{6,0},{1,3},{3,5},{5,7},{7,1},{8,10},{10,12},{12... | collective-permute-start | bytes 1572872 | tf_op jit(solution)/shard_map/ppermute | solution.py:192
  74.2 2.4 %collective-permute-start.7 = (f32[2,256,256]{2,1,0:T(8,128)}, f32[2,256,256]{2,1,0:T(8,128)S(1)}, u32[]{:S(2)}, u32[]{:S(2)}) collective-permute-start(f32[2,256,256]{2,1,0:T(8,128)} %copy-done.2), channel_id=1, source_target_pairs={{0,2},{2,4},{4,6},{6,0},{1,3},{3,5},{5,7},{7,1},{8,10},{10,12},{12... | collective-permute-start | bytes 1572872 | tf_op jit(solution)/shard_map/ppermute | solution.py:192
  76.6 3.0 %collective-permute-done.5.refs_0_ = f32[2,256,256]{2,1,0:T(8,128)S(1)} collective-permute-done((f32[2,256,256]{2,1,0:T(8,128)}, f32[2,256,256]{2,1,0:T(8,128)S(1)}, u32[]{:S(2)}, u32[]{:S(2)}) %collective-permute-start.5) | collective-permute-done | bytes 524320 | tf_op jit(solution)/shard_map/ppermute | solution.py:192
  79.6 2.1 %shard_map.79 = f32[2,256,256]{2,1,0:T(8,128)S(1)} custom-call(s32[2]{0:T(128)S(1)} %and_select_fusion.1.cols_ref, bf16[256,512]{1,0:T(8,128)(2,1)S(1)} %copy-done.1, bf16[512,4096]{1,0:T(8,128)(2,1)} %weight_ref.11, f32[2,256,256]{2,1,0:T(8,128)S(1)} %collective-permute-done.5.refs_0_), custom_call_target="tpu_custom_call" | custom-call | flops 16777216 | bytes 2097152 | tf_op jit(solution)/shard_map/pallas_call | solution.py:31
  81.7 2.3 %collective-permute-start.6 = (f32[2,256,256]{2,1,0:T(8,128)S(1)}, f32[2,256,256]{2,1,0:T(8,128)S(1)}, u32[]{:S(2)}, u32[]{:S(2)}) collective-permute-start(f32[2,256,256]{2,1,0:T(8,128)S(1)} %shard_map.79), channel_id=1, source_target_pairs={{0,6},{2,0},{4,2},{6,4},{1,7},{3,1},{5,3},{7,5},{8,14},{10,8},{12,... | collective-permute-start | bytes 1572872 | tf_op jit(solution)/shard_map/ppermute | solution.py:192
  84.1 6.7 %collective-permute-done.3.right_ref = f32[2,256,256]{2,1,0:T(8,128)S(1)} collective-permute-done((f32[2,256,256]{2,1,0:T(8,128)}, f32[2,256,256]{2,1,0:T(8,128)S(1)}, u32[]{:S(2)}, u32[]{:S(2)}) %collective-permute-start.3) | collective-permute-done | bytes 524320 | tf_op jit(solution)/shard_map/ppermute | solution.py:192
  90.8 2.2 %shard_map.77 = (f32[256,256]{1,0:T(8,128)S(1)}, f32[256,256]{1,0:T(8,128)S(1)}) custom-call(s32[3]{0:T(128)S(1)} %pad_add_fusion.1.cols_ref, bf16[256,512]{1,0:T(8,128)(2,1)S(1)} %copy-done.1, bf16[512,4096]{1,0:T(8,128)(2,1)} %weight_ref.11, f32[2,256,256]{2,1,0:T(8,128)S(1)} %collective-permute-done.2.left_ref, ...), custom_call_target="tpu_custom_call" | custom-call | flops 16777216 | bytes 2097152 | tf_op jit(solution)/shard_map/pallas_call | solution.py:31
  93.0 8.2 %collective-permute-start.4 = (f32[256,256]{1,0:T(8,128)S(1)}, f32[256,256]{1,0:T(8,128)S(1)}, u32[]{:S(2)}, u32[]{:S(2)}) collective-permute-start(f32[256,256]{1,0:T(8,128)S(1)} %get-tuple-element.28), channel_id=1, source_target_pairs={{0,1},{1,0},{2,3},{3,2},{4,5},{5,4},{6,7},{7,6},{8,9},{9,8},{10,11... | collective-permute-start | bytes 786440 | tf_op jit(solution)/shard_map/ppermute | solution.py:192
  101.4 2.2 %shard_map.80 = (f32[256,256]{1,0:T(8,128)S(1)}, f32[256,256]{1,0:T(8,128)S(1)}) custom-call(s32[3]{0:T(128)S(1)} %pad_add_fusion.5.cols_ref, bf16[256,512]{1,0:T(8,128)(2,1)S(1)} %copy-done.1, bf16[512,4096]{1,0:T(8,128)(2,1)} %weight_ref.11, f32[2,256,256]{2,1,0:T(8,128)S(1)} %collective-permute-done.6.left_ref, ...), custom_call_target="tpu_custom_call" | custom-call | flops 16777216 | bytes 2097152 | tf_op jit(solution)/shard_map/pallas_call | solution.py:31
  103.6 6.3 %collective-permute-start.8 = (f32[256,256]{1,0:T(8,128)S(1)}, f32[256,256]{1,0:T(8,128)S(1)}, u32[]{:S(2)}, u32[]{:S(2)}) collective-permute-start(f32[256,256]{1,0:T(8,128)S(1)} %get-tuple-element.32), channel_id=1, source_target_pairs={{0,1},{1,0},{2,3},{3,2},{4,5},{5,4},{6,7},{7,6},{8,9},{9,8},{10,11... | collective-permute-start | bytes 786440 | tf_op jit(solution)/shard_map/ppermute | solution.py:192
  109.9 31.3 %collective-permute-done.4 = f32[256,256]{1,0:T(8,128)S(1)} collective-permute-done((f32[256,256]{1,0:T(8,128)S(1)}, f32[256,256]{1,0:T(8,128)S(1)}, u32[]{:S(2)}, u32[]{:S(2)}) %collective-permute-start.4) | collective-permute-done | bytes 262176 | tf_op jit(solution)/shard_map/ppermute | solution.py:192
  141.3 2.8 %collective-permute-done.8 = f32[256,256]{1,0:T(8,128)S(1)} collective-permute-done((f32[256,256]{1,0:T(8,128)S(1)}, f32[256,256]{1,0:T(8,128)S(1)}, u32[]{:S(2)}, u32[]{:S(2)}) %collective-permute-start.8) | collective-permute-done | bytes 262176 | tf_op jit(solution)/shard_map/ppermute | solution.py:192
  144.1 0.7 pad_maximum_fusion
  (20 shorter events, 1.9 us)
Async XLA Ops:
  3.0 3.3 %collective-permute-start = (f32[16,512]{1,0:T(8,128)}, f32[16,512]{1,0:T(8,128)S(1)}, u32[]{:S(2)}, u32[]{:S(2)}) collective-permute-start(f32[16,512]{1,0:T(8,128)} %get-tuple-element.23), channel_id=1, source_target_pairs={{0,8},{8,0},{1,9},{9,1},{2,10},{10,2},{3,11},{11,3},{4,12},{12,4},... | collective-permute-start | bytes 98312 | tf_op jit(solution)/shard_map/ppermute | solution.py:201
  7.8 29.5 %all-to-all-start = ((f32[8,16,512]{2,1,0:T(8,128)}), f32[8,16,512]{2,1,0:T(8,128)S(1)}, u32[]{:S(2)}, u32[]{:S(2)}) async-start(f32[8,16,512]{2,1,0:T(8,128)} %broadcast_in_dim.15), calls=%async_computation | async-start | bytes 524288 | tf_op jit(solution)/shard_map/all_to_all | solution.py:205
  38.8 10.4 %all-to-all-start.1 = ((f32[4,16,512]{2,1,0:T(8,128)}), f32[4,16,512]{2,1,0:T(8,128)S(1)}, u32[]{:S(2)}, u32[]{:S(2)}) async-start(f32[4,16,512]{2,1,0:T(8,128)} %broadcast_in_dim.16), calls=%async_computation.1 | async-start | bytes 262144 | tf_op jit(solution)/shard_map/all_to_all | solution.py:205
  54.7 13.0 %collective-permute-start.1 = (f32[2,256,256]{2,1,0:T(8,128)}, f32[2,256,256]{2,1,0:T(8,128)S(1)}, u32[]{:S(2)}, u32[]{:S(2)}) collective-permute-start(f32[2,256,256]{2,1,0:T(8,128)} %get-tuple-element.25), channel_id=1, source_target_pairs={{0,2},{2,4},{4,6},{6,0},{1,3},{3,5},{5,7},{7,1},{8,10},{10,12},{12... | collective-permute-start | bytes 1572872 | tf_op jit(solution)/shard_map/ppermute | solution.py:192
  57.2 1.0 copy-start
  58.2 21.4 %copy-start.1 = (bf16[256,512]{1,0:T(8,128)(2,1)S(1)}, bf16[256,512]{1,0:T(8,128)(2,1)}, u32[]{:S(2)}) copy-start(bf16[256,512]{1,0:T(8,128)(2,1)} %get-tuple-element.24.gated_ref) | copy-start | bytes 786436
  61.4 8.4 %copy-start.2 = (f32[2,256,256]{2,1,0:T(8,128)}, f32[2,256,256]{2,1,0:T(8,128)S(1)}, u32[]{:S(2)}) copy-start(f32[2,256,256]{2,1,0:T(8,128)S(1)} %get-tuple-element.30) | copy-start | bytes 1572868
  61.4 18.2 %collective-permute-start.5 = (f32[2,256,256]{2,1,0:T(8,128)}, f32[2,256,256]{2,1,0:T(8,128)S(1)}, u32[]{:S(2)}, u32[]{:S(2)}) collective-permute-start(f32[2,256,256]{2,1,0:T(8,128)} %get-tuple-element.29), channel_id=1, source_target_pairs={{0,6},{2,0},{4,2},{6,4},{1,7},{3,1},{5,3},{7,5},{8,14},{10,8},{12,... | collective-permute-start | bytes 1572872 | tf_op jit(solution)/shard_map/ppermute | solution.py:192
  65.0 25.9 %collective-permute-start.3 = (f32[2,256,256]{2,1,0:T(8,128)}, f32[2,256,256]{2,1,0:T(8,128)S(1)}, u32[]{:S(2)}, u32[]{:S(2)}) collective-permute-start(f32[2,256,256]{2,1,0:T(8,128)} %get-tuple-element.26), channel_id=1, source_target_pairs={{0,6},{2,0},{4,2},{6,4},{1,7},{3,1},{5,3},{7,5},{8,14},{10,8},{12,... | collective-permute-start | bytes 1572872 | tf_op jit(solution)/shard_map/ppermute | solution.py:192
  69.8 21.0 %collective-permute-start.2 = (f32[2,256,256]{2,1,0:T(8,128)S(1)}, f32[2,256,256]{2,1,0:T(8,128)S(1)}, u32[]{:S(2)}, u32[]{:S(2)}) collective-permute-start(f32[2,256,256]{2,1,0:T(8,128)S(1)} %shard_map.76), channel_id=1, source_target_pairs={{0,2},{2,4},{4,6},{6,0},{1,3},{3,5},{5,7},{7,1},{8,10},{10,12},{12... | collective-permute-start | bytes 1572872 | tf_op jit(solution)/shard_map/ppermute | solution.py:192
  74.2 27.2 %collective-permute-start.7 = (f32[2,256,256]{2,1,0:T(8,128)}, f32[2,256,256]{2,1,0:T(8,128)S(1)}, u32[]{:S(2)}, u32[]{:S(2)}) collective-permute-start(f32[2,256,256]{2,1,0:T(8,128)} %copy-done.2), channel_id=1, source_target_pairs={{0,2},{2,4},{4,6},{6,0},{1,3},{3,5},{5,7},{7,1},{8,10},{10,12},{12... | collective-permute-start | bytes 1572872 | tf_op jit(solution)/shard_map/ppermute | solution.py:192
  81.7 19.7 %collective-permute-start.6 = (f32[2,256,256]{2,1,0:T(8,128)S(1)}, f32[2,256,256]{2,1,0:T(8,128)S(1)}, u32[]{:S(2)}, u32[]{:S(2)}) collective-permute-start(f32[2,256,256]{2,1,0:T(8,128)S(1)} %shard_map.79), channel_id=1, source_target_pairs={{0,6},{2,0},{4,2},{6,4},{1,7},{3,1},{5,3},{7,5},{8,14},{10,8},{12,... | collective-permute-start | bytes 1572872 | tf_op jit(solution)/shard_map/ppermute | solution.py:192
  93.0 48.3 %collective-permute-start.4 = (f32[256,256]{1,0:T(8,128)S(1)}, f32[256,256]{1,0:T(8,128)S(1)}, u32[]{:S(2)}, u32[]{:S(2)}) collective-permute-start(f32[256,256]{1,0:T(8,128)S(1)} %get-tuple-element.28), channel_id=1, source_target_pairs={{0,1},{1,0},{2,3},{3,2},{4,5},{5,4},{6,7},{7,6},{8,9},{9,8},{10,11... | collective-permute-start | bytes 786440 | tf_op jit(solution)/shard_map/ppermute | solution.py:192
  103.6 40.5 %collective-permute-start.8 = (f32[256,256]{1,0:T(8,128)S(1)}, f32[256,256]{1,0:T(8,128)S(1)}, u32[]{:S(2)}, u32[]{:S(2)}) collective-permute-start(f32[256,256]{1,0:T(8,128)S(1)} %get-tuple-element.32), channel_id=1, source_target_pairs={{0,1},{1,0},{2,3},{3,2},{4,5},{5,4},{6,7},{7,6},{8,9},{9,8},{10,11... | collective-permute-start | bytes 786440 | tf_op jit(solution)/shard_map/ppermute | solution.py:192
